TPU v7x, 512 devices: a whole 4x4x16 slice. The times are simulated.
512 devices in a mesh: seq: 64 (over y_hi, z, core), chan: 8 (over x, y_lo).
Axes of the slice: x: 4, y: 4 (y_hi: 2, y_lo: 2; y = y_hi * 2 + y_lo), z: 16, core: 2. Of those that a mesh axis runs over, the one named last changes fastest.
Arguments:
- query_gate: bfloat16 [8192, 8192], P('seq', 'chan'), may hold values from -6 to 6
- key_gate: bfloat16 [8192, 8192], P('seq', 'chan'), may hold values from -6 to 6
- value_input: bfloat16 [8192, 8192], P('seq', 'chan'), may hold values from -6 to 6
- grad_out: bfloat16 [8192, 8192], P('seq', 'chan'), may hold values from -6 to 6
- residues: float32 [8192, 16], P(('chan', 'seq')), may hold values from -1.5 to 1.5
- decay: float32 [8192, 16], P(('chan', 'seq')), as said below
Outputs:
- grad_query: bfloat16 [8192, 8192], P('seq', 'chan')
- grad_key: bfloat16 [8192, 8192], P('seq', 'chan')
- grad_value: bfloat16 [8192, 8192], P('seq', 'chan')
- grad_residues: float32 [8192, 16], P(('chan', 'seq'))
Inputs may be any that keep to these rules, and one draw needn't show every extreme that they name: `decay`: positive rates, none above 0.1.
All inputs are finite; a program needn't handle non-finite values.
Results may differ from a plain program's by a relative error of at most 0.011.
Values may be sent and summed in bfloat16 or wider, within the bound.
A program may use at most 128 MiB of HBM per device.

v0:
```python
import math

import jax
import jax.numpy as jnp
from jax import lax
from jax.sharding import PartitionSpec as P

HIGH = lax.Precision.HIGHEST


def block_size(length, channels):
    blk = min(length, 128)
    while blk > 8 and channels * blk * blk > 262144:
        blk = blk // 2
    return blk


def link(earlier, later):
    return (earlier[0] * later[0], later[0] * earlier[1] + later[1])


def toeplitz(taps):
    channels, blk = taps.shape
    cycle = jnp.concatenate(
        [taps[:, :1], jnp.zeros((channels, blk - 1), taps.dtype), jnp.flip(taps[:, 1:], axis=1)],
        axis=1,
    )
    flat = jnp.tile(cycle, (1, blk))[:, : blk * (2 * blk - 2)]
    return flat.reshape(channels, blk, 2 * blk - 2)[:, :, :blk]


def lag_sums(pairs):
    channels, blk, _ = pairs.shape
    wide = jnp.pad(pairs, ((0, 0), (0, 0), (0, blk)))
    flat = jnp.pad(wide.reshape(channels, 2 * blk * blk), ((0, 0), (0, blk)))
    skewed = flat.reshape(channels, blk, 2 * blk + 1)
    return jnp.sum(skewed[:, :, :blk], axis=1)


def prepare(conv_input, conv_grad, decay):
    length, channels = conv_input.shape
    blk = block_size(length, channels)
    count = length // blk
    position = jnp.arange(blk, dtype=jnp.float32)
    lags = jnp.exp(-decay[:, :, None] * position)
    lead = lags * jnp.exp(-decay)[:, :, None]
    inputs = conv_input.reshape(count, blk, channels)
    grads = conv_grad.reshape(count, blk, channels)
    ends = jnp.einsum("bjc,cmj->bcm", inputs, jnp.flip(lags, axis=2), precision=HIGH)
    starts = jnp.einsum("bjc,cmj->bcm", grads, lags, precision=HIGH)
    step = jnp.broadcast_to(jnp.exp(-decay * blk)[None], ends.shape)
    carried = lax.associative_scan(link, (step, ends), axis=0)[1]
    returned = lax.associative_scan(link, (step, starts), reverse=True, axis=0)[1]
    nothing = jnp.zeros_like(ends[:1])
    before = jnp.concatenate([nothing, carried[:-1]], axis=0)
    after = jnp.concatenate([returned[1:], nothing], axis=0)
    powers = jnp.exp(-decay[None] * (blk * jnp.arange(count, dtype=jnp.float32))[:, None, None])
    return (inputs, grads, lags, lead, before, after, powers, carried[-1], returned[0])


def finish(parts, gain, entry, leaving):
    inputs, grads, lags, lead, before, after, powers, last_state, first_state = parts
    count, blk, channels = inputs.shape
    before = before + powers * entry[None]
    after = after + jnp.flip(powers, axis=0) * leaving[None]
    taps = jnp.einsum("cm,cmd->cd", gain, lags, precision=HIGH)
    kernel = toeplitz(taps)
    output = jnp.einsum("cij,bjc->bic", kernel, inputs, precision=HIGH)
    output = output + jnp.einsum("bcm,cmi->bic", before * gain[None], lead, precision=HIGH)
    backward = jnp.einsum("cji,bjc->bic", kernel, grads, precision=HIGH)
    backward = backward + jnp.einsum(
        "bcm,cmi->bic", after * gain[None], jnp.flip(lead, axis=2), precision=HIGH
    )
    pairs = jnp.einsum("bjc,bic->cji", inputs, grads, precision=HIGH)
    inner = jnp.einsum("cd,cmd->cm", lag_sums(pairs), lags, precision=HIGH)
    reach = jnp.einsum("bic,cmi->bcm", grads, lead, precision=HIGH)
    score = inner + jnp.sum(before * reach, axis=0)
    return (output.reshape(count * blk, channels), backward.reshape(count * blk, channels), score)


def gated(left, right):
    return (left.astype(jnp.float32) * right.astype(jnp.float32)).astype(jnp.bfloat16)


def widen(first, second):
    first, second = lax.optimization_barrier((first, second))
    return (first.astype(jnp.float32), second.astype(jnp.float32))


def body(query_gate, key_gate, value_input, grad_out, residues, decay):
    length = query_gate.shape[0] * lax.axis_size("seq")
    factor = 1.0 / math.sqrt(length)
    mode_scale = jnp.sqrt(1.0 - jnp.exp(-2.0 * decay))
    moved_query, moved_key, moved_value, moved_out = (
        lax.all_to_all(query_gate, "seq", split_axis=1, concat_axis=0, tiled=True),
        lax.all_to_all(key_gate, "seq", split_axis=1, concat_axis=0, tiled=True),
        lax.all_to_all(value_input, "seq", split_axis=1, concat_axis=0, tiled=True),
        lax.all_to_all(grad_out, "seq", split_axis=1, concat_axis=0, tiled=True),
    )
    moved_input = gated(moved_key, moved_value)
    moved_grad = gated(moved_out, moved_query)
    input_f, grad_f = widen(moved_input, moved_grad)
    parts = prepare(input_f, grad_f, decay)
    empty = jnp.zeros_like(decay)
    output, backward, score = finish(parts, residues * mode_scale, empty, empty)
    output_b = output.astype(jnp.bfloat16)
    backward_b = backward.astype(jnp.bfloat16)
    grad_query, grad_key, grad_value = (
        lax.all_to_all(gated(moved_out, output_b), "seq", split_axis=0, concat_axis=1, tiled=True),
        lax.all_to_all(
            gated(backward_b, moved_value), "seq", split_axis=0, concat_axis=1, tiled=True
        ),
        lax.all_to_all(
            gated(backward_b, moved_key), "seq", split_axis=0, concat_axis=1, tiled=True
        ),
    )
    grad_residues = mode_scale * score * factor
    return (grad_query, grad_key, grad_value, grad_residues)


def solution(mesh):
    return jax.shard_map(
        body,
        mesh=mesh,
        in_specs=(
            P("seq", "chan"),
            P("seq", "chan"),
            P("seq", "chan"),
            P("seq", "chan"),
            P(("chan", "seq"), None),
            P(("chan", "seq"), None),
        ),
        out_specs=(P("seq", "chan"), P("seq", "chan"), P("seq", "chan"), P(("chan", "seq"), None)),
        check_vma=False,
    )
```

profile of v0, /device:TPU:1, one launch (start us, length us, event | category | flops | bytes accessed | tf_op | source)
XLA Modules:
  0.0 317.9 jit_solution(10105821423209699034)
XLA Ops:
  2.5 19.8 %all-to-all-start.3 = ((bf16[128,64,16]{0,2,1:T(8,128)(2,1)}), bf16[128,64,16]{0,2,1:T(8,128)(2,1)S(1)}, u32[]{:S(2)}, u32[]{:S(2)}) async-start(bf16[128,64,16]{0,2,1:T(8,128)(2,1)} %bitcast.5), calls=%async_computation.3 | async-start | bytes 524288 | tf_op jit(solution)/shard_map/all_to_all | solution.py:95
  24.1 22.0 %all-to-all-done.3 = bf16[128,64,16]{0,2,1:T(8,128)(2,1)S(1)} async-done(((bf16[128,64,16]{0,2,1:T(8,128)(2,1)}), bf16[128,64,16]{0,2,1:T(8,128)(2,1)S(1)}, u32[]{:S(2)}, u32[]{:S(2)}) %all-to-all-start.3) | async-done | bytes 262176 | tf_op jit(solution)/shard_map/all_to_all | solution.py:95
  46.0 4.2 %all-to-all-start = ((bf16[128,64,16]{0,2,1:T(8,128)(2,1)}), bf16[128,64,16]{0,2,1:T(8,128)(2,1)S(1)}, u32[]{:S(2)}, u32[]{:S(2)}) async-start(bf16[128,64,16]{0,2,1:T(8,128)(2,1)} %bitcast), calls=%async_computation | async-start | bytes 524288 | tf_op jit(solution)/shard_map/all_to_all | solution.py:98
  51.1 22.7 %all-to-all-done = bf16[128,64,16]{0,2,1:T(8,128)(2,1)S(1)} async-done(((bf16[128,64,16]{0,2,1:T(8,128)(2,1)}), bf16[128,64,16]{0,2,1:T(8,128)(2,1)S(1)}, u32[]{:S(2)}, u32[]{:S(2)}) %all-to-all-start) | async-done | bytes 262176 | tf_op jit(solution)/shard_map/all_to_all | solution.py:98
  73.8 4.2 %all-to-all-start.2 = ((bf16[128,64,16]{0,2,1:T(8,128)(2,1)}), bf16[128,64,16]{0,2,1:T(8,128)(2,1)S(1)}, u32[]{:S(2)}, u32[]{:S(2)}) async-start(bf16[128,64,16]{0,2,1:T(8,128)(2,1)} %bitcast.3), calls=%async_computation.2 | async-start | bytes 524288 | tf_op jit(solution)/shard_map/all_to_all | solution.py:97
  78.9 22.7 %all-to-all-done.2 = bf16[128,64,16]{0,2,1:T(8,128)(2,1)S(1)} async-done(((bf16[128,64,16]{0,2,1:T(8,128)(2,1)}), bf16[128,64,16]{0,2,1:T(8,128)(2,1)S(1)}, u32[]{:S(2)}, u32[]{:S(2)}) %all-to-all-start.2) | async-done | bytes 262176 | tf_op jit(solution)/shard_map/all_to_all | solution.py:97
  101.6 4.4 %all-to-all-start.1 = ((bf16[128,64,16]{0,2,1:T(8,128)(2,1)}), bf16[128,64,16]{0,2,1:T(8,128)(2,1)S(1)}, u32[]{:S(2)}, u32[]{:S(2)}) async-start(bf16[128,64,16]{0,2,1:T(8,128)(2,1)} %bitcast.2), calls=%async_computation.1 | async-start | bytes 524288 | tf_op jit(solution)/shard_map/all_to_all | solution.py:96
  112.0 17.5 %all-to-all-done.1 = bf16[128,64,16]{0,2,1:T(8,128)(2,1)S(1)} async-done(((bf16[128,64,16]{0,2,1:T(8,128)(2,1)}), bf16[128,64,16]{0,2,1:T(8,128)(2,1)S(1)}, u32[]{:S(2)}, u32[]{:S(2)}) %all-to-all-start.1) | async-done | bytes 262176 | tf_op jit(solution)/shard_map/all_to_all | solution.py:96
  130.5 1.9 slice.334
  169.5 3.6 %reshape.75 = f32[16,128,257]{2,1,0:T(8,128)} reshape(f32[16,32896]{1,0:T(8,128)S(1)} %pad.109) | data formatting | bytes 4210688 | tf_op jit(solution)/shard_map/reshape | solution.py:36
  189.1 2.1 pad.135
  191.3 2.2 pad.169
  195.4 2.5 tile.10
  197.9 3.1 slice.386
  201.0 4.8 %reshape.72 = f32[16,128,254]{2,1,0:T(8,128)S(1)} reshape(f32[16,32512]{1,0:T(8,128)} %slice.386) | data formatting | bytes 4161536 | tf_op jit(solution)/shard_map/reshape | solution.py:29
  209.0 4.5 %all-to-all-start.4 = ((bf16[64,128,16]{1,2,0:T(8,128)(2,1)}), bf16[64,128,16]{1,2,0:T(8,128)(2,1)S(1)}, u32[]{:S(2)}, u32[]{:S(2)}) async-start(bf16[64,128,16]{1,2,0:T(8,128)(2,1)} %copy.81), calls=%async_computation.4 | async-start | bytes 524288 | tf_op jit(solution)/shard_map/all_to_all | solution.py:109
  217.3 6.2 %pad.99 = f32[4,16,16]{0,2,1:T(8,128)S(1)} pad(f32[2,16,16]{0,2,1:T(8,128)} %pad_add_fusion, f32[]{:T(128)} %constant.7.clone.1), padding=1_0_1x0_0_0x0_0_0 | pad | bytes 6148 | tf_op jit(solution)/shard_map/pad | solution.py:53
  238.1 2.1 pad.137
  240.2 6.8 %pad.170 = f32[64,16,16]{0,2,1:T(8,128)S(1)} pad(f32[32,16,16]{0,2,1:T(8,128)} %add.206, f32[]{:T(128)} %constant.7.clone.1), padding=1_0_1x0_0_0x0_0_0 | pad | bytes 98308
  247.7 2.1 fusion.13
  250.8 14.8 %all-to-all-start.5 = ((bf16[64,128,16]{1,2,0:T(8,128)(2,1)}), bf16[64,128,16]{1,2,0:T(8,128)(2,1)S(1)}, u32[]{:S(2)}, u32[]{:S(2)}) async-start(bf16[64,128,16]{1,2,0:T(8,128)(2,1)} %copy.82), calls=%async_computation.5 | async-start | bytes 524288 | tf_op jit(solution)/shard_map/all_to_all | solution.py:110
  266.4 22.9 %all-to-all-done.5 = bf16[64,128,16]{1,2,0:T(8,128)(2,1)S(1)} async-done(((bf16[64,128,16]{1,2,0:T(8,128)(2,1)}), bf16[64,128,16]{1,2,0:T(8,128)(2,1)S(1)}, u32[]{:S(2)}, u32[]{:S(2)}) %all-to-all-start.5) | async-done | bytes 262176 | tf_op jit(solution)/shard_map/all_to_all | solution.py:110
  289.3 4.2 %all-to-all-start.6 = ((bf16[64,128,16]{1,2,0:T(8,128)(2,1)}), bf16[64,128,16]{1,2,0:T(8,128)(2,1)S(1)}, u32[]{:S(2)}, u32[]{:S(2)}) async-start(bf16[64,128,16]{1,2,0:T(8,128)(2,1)} %copy.83), calls=%async_computation.6 | async-start | bytes 524288 | tf_op jit(solution)/shard_map/all_to_all | solution.py:113
  295.2 21.9 %all-to-all-done.6 = bf16[64,128,16]{1,2,0:T(8,128)(2,1)S(1)} async-done(((bf16[64,128,16]{1,2,0:T(8,128)(2,1)}), bf16[64,128,16]{1,2,0:T(8,128)(2,1)S(1)}, u32[]{:S(2)}, u32[]{:S(2)}) %all-to-all-start.6) | async-done | bytes 262176 | tf_op jit(solution)/shard_map/all_to_all | solution.py:113
  (213 shorter events, 93.1 us)
Async XLA Ops:
  0.6 49.6 %copy-start.13 = (bf16[128,1024]{1,0:T(8,128)(2,1)S(1)}, bf16[128,1024]{1,0:T(8,128)(2,1)}, u32[]{:S(2)}) copy-start(bf16[128,1024]{1,0:T(8,128)(2,1)} %param.8) | copy-start | bytes 786436
  0.6 77.4 %copy-start.14 = (bf16[128,1024]{1,0:T(8,128)(2,1)S(1)}, bf16[128,1024]{1,0:T(8,128)(2,1)}, u32[]{:S(2)}) copy-start(bf16[128,1024]{1,0:T(8,128)(2,1)} %param.7) | copy-start | bytes 786436
  0.7 105.4 %copy-start.25 = (f32[16,16]{1,0:T(8,128)S(1)}, f32[16,16]{1,0:T(8,128)}, u32[]{:S(2)}) copy-start(f32[16,16]{1,0:T(8,128)} %param.11) | copy-start | bytes 3076
  2.5 43.5 %all-to-all-start.3 = ((bf16[128,64,16]{0,2,1:T(8,128)(2,1)}), bf16[128,64,16]{0,2,1:T(8,128)(2,1)S(1)}, u32[]{:S(2)}, u32[]{:S(2)}) async-start(bf16[128,64,16]{0,2,1:T(8,128)(2,1)} %bitcast.5), calls=%async_computation.3 | async-start | bytes 524288 | tf_op jit(solution)/shard_map/all_to_all | solution.py:95
  46.0 27.8 %all-to-all-start = ((bf16[128,64,16]{0,2,1:T(8,128)(2,1)}), bf16[128,64,16]{0,2,1:T(8,128)(2,1)S(1)}, u32[]{:S(2)}, u32[]{:S(2)}) async-start(bf16[128,64,16]{0,2,1:T(8,128)(2,1)} %bitcast), calls=%async_computation | async-start | bytes 524288 | tf_op jit(solution)/shard_map/all_to_all | solution.py:98
  73.8 38.1 %copy-start.6 = (bf16[128,64,16]{0,2,1:T(8,128)(2,1)}, bf16[128,64,16]{0,2,1:T(8,128)(2,1)S(1)}, u32[]{:S(2)}) copy-start(bf16[128,64,16]{0,2,1:T(8,128)(2,1)S(1)} %all-to-all-done) | copy-start | bytes 786436
  73.8 27.8 %all-to-all-start.2 = ((bf16[128,64,16]{0,2,1:T(8,128)(2,1)}), bf16[128,64,16]{0,2,1:T(8,128)(2,1)S(1)}, u32[]{:S(2)}, u32[]{:S(2)}) async-start(bf16[128,64,16]{0,2,1:T(8,128)(2,1)} %bitcast.3), calls=%async_computation.2 | async-start | bytes 524288 | tf_op jit(solution)/shard_map/all_to_all | solution.py:97
  101.6 27.9 %copy-start.2 = (bf16[128,64,16]{0,2,1:T(8,128)(2,1)}, bf16[128,64,16]{0,2,1:T(8,128)(2,1)S(1)}, u32[]{:S(2)}) copy-start(bf16[128,64,16]{0,2,1:T(8,128)(2,1)S(1)} %all-to-all-done.2) | copy-start | bytes 786436
  101.6 27.8 %all-to-all-start.1 = ((bf16[128,64,16]{0,2,1:T(8,128)(2,1)}), bf16[128,64,16]{0,2,1:T(8,128)(2,1)S(1)}, u32[]{:S(2)}, u32[]{:S(2)}) async-start(bf16[128,64,16]{0,2,1:T(8,128)(2,1)} %bitcast.2), calls=%async_computation.1 | async-start | bytes 524288 | tf_op jit(solution)/shard_map/all_to_all | solution.py:96
  106.7 23.2 %copy-start.17 = (f32[16,16]{1,0:T(8,128)}, f32[16,16]{1,0:T(8,128)S(1)}, u32[]{:S(2)}) copy-start(f32[16,16]{1,0:T(8,128)S(1)} %get-tuple-element.52) | copy-start | bytes 3076
  106.7 28.2 %copy-start.15 = (f32[16,16]{1,0:T(8,128)}, f32[16,16]{1,0:T(8,128)S(1)}, u32[]{:S(2)}) copy-start(f32[16,16]{1,0:T(8,128)S(1)} %get-tuple-element.53) | copy-start | bytes 3076
  106.7 29.8 %copy-start.19 = (f32[16,16]{1,0:T(8,128)}, f32[16,16]{1,0:T(8,128)S(1)}, u32[]{:S(2)}) copy-start(f32[16,16]{1,0:T(8,128)S(1)} %get-tuple-element.47) | copy-start | bytes 3076
  106.7 31.8 %copy-start.21 = (f32[16,16]{1,0:T(8,128)}, f32[16,16]{1,0:T(8,128)S(1)}, u32[]{:S(2)}) copy-start(f32[16,16]{1,0:T(8,128)S(1)} %get-tuple-element.48) | copy-start | bytes 3076
  106.7 32.6 %copy-start.23 = (f32[16,16]{1,0:T(8,128)}, f32[16,16]{1,0:T(8,128)S(1)}, u32[]{:S(2)}) copy-start(f32[16,16]{1,0:T(8,128)S(1)} %get-tuple-element.50) | copy-start | bytes 3076
  185.3 8.1 %copy-start.18 = (f32[16,16]{1,0:T(8,128)S(1)}, f32[16,16]{1,0:T(8,128)}, u32[]{:S(2)}) copy-start(f32[16,16]{1,0:T(8,128)} %copy-done.17) | copy-start | bytes 3076
  185.3 8.1 %copy-start.30 = (f32[64]{0:T(128)S(1)}, f32[64]{0:T(128)}, u32[]{:S(2)}) copy-start(f32[64]{0:T(128)} %copy-done.29) | copy-start | bytes 772
  185.4 8.7 %copy-start.26 = (f32[16,16]{1,0:T(8,128)S(1)}, f32[16,16]{1,0:T(8,128)}, u32[]{:S(2)}) copy-start(f32[16,16]{1,0:T(8,128)} %param.11) | copy-start | bytes 3076
  185.4 8.7 %copy-start.27 = (f32[16,16]{1,0:T(8,128)S(1)}, f32[16,16]{1,0:T(8,128)}, u32[]{:S(2)}) copy-start(f32[16,16]{1,0:T(8,128)} %param.10) | copy-start | bytes 3076
  187.1 8.2 %copy-start.28 = (f32[255]{0:T(256)S(1)}, f32[255]{0:T(256)}, u32[]{:S(2)}) copy-start(f32[255]{0:T(256)} %pad.133.clone) | copy-start | bytes 3064
  209.0 41.8 %all-to-all-start.4 = ((bf16[64,128,16]{1,2,0:T(8,128)(2,1)}), bf16[64,128,16]{1,2,0:T(8,128)(2,1)S(1)}, u32[]{:S(2)}, u32[]{:S(2)}) async-start(bf16[64,128,16]{1,2,0:T(8,128)(2,1)} %copy.81), calls=%async_computation.4 | async-start | bytes 524288 | tf_op jit(solution)/shard_map/all_to_all | solution.py:109
  236.0 11.7 %copy-start.3 = (bf16[128,64,16]{0,2,1:T(8,128)(2,1)S(1)}, bf16[128,64,16]{0,2,1:T(8,128)(2,1)}, u32[]{:S(2)}) copy-start(bf16[128,64,16]{0,2,1:T(8,128)(2,1)} %copy-done.2) | copy-start | bytes 786436
  236.0 11.8 %copy-start.5 = (bf16[128,64,16]{0,2,1:T(8,128)(2,1)S(1)}, bf16[128,64,16]{0,2,1:T(8,128)(2,1)}, u32[]{:S(2)}) copy-start(bf16[128,64,16]{0,2,1:T(8,128)(2,1)} %copy-done.4) | copy-start | bytes 786436
  250.8 38.5 %all-to-all-start.5 = ((bf16[64,128,16]{1,2,0:T(8,128)(2,1)}), bf16[64,128,16]{1,2,0:T(8,128)(2,1)S(1)}, u32[]{:S(2)}, u32[]{:S(2)}) async-start(bf16[64,128,16]{1,2,0:T(8,128)(2,1)} %copy.82), calls=%async_computation.5 | async-start | bytes 524288 | tf_op jit(solution)/shard_map/all_to_all | solution.py:110
  289.3 27.8 %all-to-all-start.6 = ((bf16[64,128,16]{1,2,0:T(8,128)(2,1)}), bf16[64,128,16]{1,2,0:T(8,128)(2,1)S(1)}, u32[]{:S(2)}, u32[]{:S(2)}) async-start(bf16[64,128,16]{1,2,0:T(8,128)(2,1)} %copy.83), calls=%async_computation.6 | async-start | bytes 524288 | tf_op jit(solution)/shard_map/all_to_all | solution.py:113
  (14 other events, 80.2 us)
where the time goes:
time: 320 us; the launch traced here: 318 us
  waiting for transfers between devices  130 us (41%)
  local copies, waits for them, and re-layouts  105 us (33%)
  starting transfers between devices  56 us (18%)
  other arithmetic  17.7 us (6%)
  matrix products  7.92 us (2%)
    all_to_all x1, waiting for transfers between devices, body(): lax.all_to_all(gated(backward_b, moved_value), 'seq', split_axis=0, conca...  22.9 us
    all_to_all x1, waiting for transfers between devices, body(): lax.all_to_all(grad_out, 'seq', split_axis=1, concat_axis=0, tiled=True)  22.7 us
    all_to_all x1, waiting for transfers between devices, body(): lax.all_to_all(value_input, 'seq', split_axis=1, concat_axis=0, tiled=True)  22.7 us
    slice x31, local copies, waits for them, and re-layouts, prepare(): lax.associative_scan(link, (step, starts), reverse=True, axis=0)[1]  22.3 us
    all_to_all x1, waiting for transfers between devices, body(): lax.all_to_all(query_gate, 'seq', split_axis=1, concat_axis=0, tiled=True)  22 us
    all_to_all x1, waiting for transfers between devices, body(): lax.all_to_all(gated(backward_b, moved_key), 'seq', split_axis=0, concat_...  21.9 us
    all_to_all x1, starting transfers between devices, body(): lax.all_to_all(query_gate, 'seq', split_axis=1, concat_axis=0, tiled=True)  19.8 us
    unnamed x74, local copies, waits for them, and re-layouts  18.2 us
  transfers between devices with their start and end apart: 7, of which 6 were waited for; matrix products, arithmetic and copies ran while one was open for 15% of the time, Pallas kernels for 0%

commit v1 on v0

v1 whole, which is shorter than its diff:
```python
import functools
import math

import jax
import jax.numpy as jnp
import ml_dtypes
import numpy as np
from jax import lax
from jax.experimental import pallas as pl
from jax.experimental.pallas import tpu as pltpu
from jax.sharding import PartitionSpec as P

MESH = pl.DeviceIdType.MESH
F32 = jnp.float32
BF16 = jnp.bfloat16
SPAN = 128
NODES = 16
MODES = 16
BLOCKS = 8
CHUNKS = 64
OWN = 16
Z_FIRST, Z_STEP = 12, 1


def scan_device(block, core):
    z = (Z_FIRST + Z_STEP * (block % 4)) % 16
    return (block // 4) * 32 + z * 2 + core


def nodes():
    k = np.arange(NODES)
    half = (SPAN - 1) / 2.0
    return half + half * np.cos(np.pi * (2 * k + 1) / (2 * NODES))


def cardinal():
    t = nodes()
    lag = np.arange(SPAN, dtype=np.float64)
    out = np.ones((NODES, SPAN))
    for k in range(NODES):
        for j in range(NODES):
            if j != k:
                out[k] *= (lag - t[j]) / (t[k] - t[j])
    return out


def split(a):
    high = a.astype(ml_dtypes.bfloat16)
    low = (a - high.astype(np.float64)).astype(ml_dtypes.bfloat16)
    return np.concatenate([high, low], axis=-1)


@functools.cache
def tables():
    phi = cardinal()
    t = np.arange(SPAN)
    lag = t[:, None] - t[None, :]
    inside = lag >= 0
    low = np.where(inside[None], phi[:, np.where(inside, lag, 0)], 0.0)
    forward = low.reshape(NODES * SPAN, SPAN)
    backward = low.transpose(0, 2, 1).reshape(NODES * SPAN, SPAN)
    toeplitz = np.stack([split(forward), split(backward)])
    moments = np.stack([split(phi[:, ::-1]), split(phi)])
    spread = np.stack([split(phi.T), split(phi[:, ::-1].T)])
    return toeplitz, moments, spread


def falling(u):
    total = jnp.full_like(u, -1.0 / 5040.0)
    for c in (720.0, -120.0, 24.0, -6.0, 2.0, -1.0):
        total = total * u - 1.0 / c
    return total * u


def kernel(
    q_hbm, k_hbm, v_hbm, go_hbm, res_hbm, dec_hbm, toe_hbm, mom_hbm, spr_hbm,
    y_out, r_out, s_out,
    q_in, k_in, v_in, go_in, res_in, dec_in, toe, mom, spr,
    x2, g2, prod, inn, y_acc, r_acc,
    mom_send, inn_send, prm_send,
    mom_rcv, inn_rcv, prm_rcv, kap_rcv, ent_rcv, sco_rcv, sib_rcv,
    psi, push, ebuf, before, ent_send, kap_send, sco_send,
    in_sem, send_sem, recv_sem,
):
    me = lax.axis_index("seq")
    core = lax.rem(me, 2)
    z = lax.rem(lax.div(me, 2), 16)
    y_hi = lax.div(me, 32)
    ahead = lax.rem(z - Z_FIRST + 16, 16)
    scans = jnp.logical_and(lax.rem(ahead, Z_STEP) == 0, ahead < 4 * Z_STEP)
    block = y_hi * 4 + lax.rem(lax.div(ahead, Z_STEP), 4)
    own_block, own_part = lax.div(me, 8), lax.rem(me, 8)
    scanners = [(b, c, scan_device(b, c)) for b in range(BLOCKS) for c in range(2)]

    loads = [
        pltpu.make_async_copy(src, dst, in_sem.at[n])
        for n, (src, dst) in enumerate(
            [
                (k_hbm, k_in), (v_hbm, v_in), (go_hbm, go_in), (q_hbm, q_in),
                (mom_hbm, mom), (res_hbm, res_in), (dec_hbm, dec_in), (spr_hbm, spr), (toe_hbm, toe),
            ]
        )
    ]
    for load in loads:
        load.start()

    barrier = pltpu.get_barrier_semaphore()

    def greet(device):
        pl.semaphore_signal(barrier, inc=1, device_id={"seq": device}, device_id_type=MESH)

    @pl.when(scans)
    def _():
        def one(n, carry):
            greet(lax.rem(me + n, CHUNKS))
            return carry

        lax.fori_loop(1, CHUNKS, one, 0)

    @pl.when(jnp.logical_not(scans))
    def _():
        for _, _, device in scanners:
            greet(device)

    for n in (0, 1, 2, 3, 4):
        loads[n].wait()
    x = (k_in[...].astype(F32) * v_in[...].astype(F32)).astype(BF16)
    g = (go_in[...].astype(F32) * q_in[...].astype(F32)).astype(BF16)
    x2[:SPAN, :] = x
    x2[SPAN:, :] = x
    g2[:SPAN, :] = g
    g2[SPAN:, :] = g
    for c, ref in ((0, x2), (1, g2)):
        value = jnp.dot(mom[c], ref[...], preferred_element_type=F32).astype(BF16)
        for b in range(BLOCKS):
            mom_send[c, b] = value[:, b * SPAN : (b + 1) * SPAN]

    loads[5].wait()
    loads[6].wait()
    lane16 = lax.broadcasted_iota(jnp.int32, (OWN, SPAN), 1)
    row16 = lax.broadcasted_iota(jnp.int32, (OWN, SPAN), 0)
    for n, ref in ((0, dec_in), (1, res_in)):
        value = ref[...]
        for r in range(2):
            wide = jnp.zeros((OWN, SPAN), F32)
            for j in range(8):
                column = jnp.broadcast_to(value[:, 8 * r + j : 8 * r + j + 1], (OWN, SPAN))
                wide = jnp.where(lane16 // 16 == j, column, wide)
            wide = jnp.where(lane16 % 16 == row16, wide, 0.0)
            prm_send[2 * n + r : 2 * n + r + 1, :] = jnp.sum(wide, axis=0, keepdims=True)

    @pl.when(scans)
    def _():
        pl.semaphore_wait(barrier, CHUNKS - 1)

    @pl.when(jnp.logical_not(scans))
    def _():
        pl.semaphore_wait(barrier, 2 * BLOCKS)

    def push_to(src, dst, kind, device):
        return pltpu.make_async_remote_copy(
            src_ref=src, dst_ref=dst, send_sem=send_sem.at[kind], recv_sem=recv_sem.at[kind],
            device_id={"seq": device}, device_id_type=MESH,
        )

    def send(src, dst, kind, device):
        @pl.when(me != device)
        def _():
            push_to(src, dst, kind, device).start()

        @pl.when(me == device)
        def _():
            pltpu.make_async_copy(src, dst, recv_sem.at[kind]).start()

    def sent(src, dst, kind, device):
        @pl.when(me != device)
        def _():
            push_to(src, dst, kind, device).wait_send()

    def arrived(ref, kind):
        pltpu.make_async_copy(ref, ref, recv_sem.at[kind]).wait()

    MOM, INN, PRM, KAP, ENT, SCO, SIB = range(7)
    moment_args = [(mom_send.at[c, b], mom_rcv.at[me], MOM, device) for b, c, device in scanners]
    inner_args = [(inn_send.at[b], inn_rcv.at[me], INN, device) for b, c, device in scanners if c == 0]
    for args in moment_args:
        send(*args)
    own_scan = [
        lax.div(own_block, 4) * 32
        + lax.rem(Z_FIRST + Z_STEP * lax.rem(own_block, 4), 16) * 2
        + c
        for c in range(2)
    ]
    param_args = [(prm_send, prm_rcv.at[own_part], PRM, device) for device in own_scan]
    for args in param_args:
        send(*args)

    loads[7].wait()
    loads[8].wait()

    def local(j, carry):
        cols = pl.ds(pl.multiple_of(j * 256, 256), 256)
        prod[0, :, cols] = jnp.dot(toe[0], x2[:, cols], preferred_element_type=F32)
        prod[1, :, cols] = jnp.dot(toe[1], g2[:, cols], preferred_element_type=F32)
        grad = g2[:SPAN, cols].astype(F32)
        for k in range(NODES):
            inn[k : k + 1, cols] = jnp.sum(
                prod[0, k * SPAN : (k + 1) * SPAN, cols] * grad, axis=0, keepdims=True
            )
        return carry

    lax.fori_loop(0, 4, local, 0)
    for b in range(BLOCKS):
        inn_send[b] = inn[:, b * SPAN : (b + 1) * SPAN].astype(BF16)
    for args in inner_args:
        send(*args)

    def chunk_at(i):
        return i + core * (CHUNKS - 1 - 2 * i)

    @pl.when(scans)
    def _():
        arrived(prm_rcv, PRM)
        lane8 = lax.broadcasted_iota(jnp.int32, (8, SPAN), 1)
        row8 = lax.broadcasted_iota(jnp.int32, (8, SPAN), 0)
        halves = []
        for r in range(4):
            packed = jnp.concatenate([prm_rcv[k, r : r + 1, :] for k in range(8)], axis=0)
            skewed = pltpu.roll(packed, 0, 1, stride=16, stride_axis=0)
            out = jnp.zeros((8, SPAN), F32)
            for j in range(8):
                turned = pltpu.roll(skewed, (SPAN - 16 * j) % SPAN, 1)
                turned = jnp.where(lane8 // 16 == row8, turned, 0.0)
                out = jnp.where(row8 == j, jnp.sum(turned, axis=0, keepdims=True), out)
            halves.append(out)
        decay = jnp.concatenate(halves[:2], axis=0)
        residue = jnp.concatenate(halves[2:], axis=0)
        scale = jnp.sqrt(falling(2.0 * decay))
        gain = residue * scale
        keep = 1.0 - falling(decay)
        points = nodes()
        for k in range(NODES):
            psi[k] = jnp.exp(decay * float(-points[k]))
        where = jnp.zeros((NODES, SPAN), F32)
        rows = lax.broadcasted_iota(jnp.int32, (NODES, SPAN), 0)
        for k in range(NODES):
            where = jnp.where(rows == k, float(-points[k]), where)
        kappa = jnp.zeros((NODES, SPAN), F32)
        for m in range(MODES):
            wave = jnp.exp(where * decay[m : m + 1, :]) * gain[m : m + 1, :]
            kappa = kappa + wave
            push[m] = wave * keep[m : m + 1, :]
        kap_send[...] = kappa

        def tell(n, carry):
            send(kap_send, kap_rcv.at[block], KAP, 2 * n + core)
            return carry

        lax.fori_loop(0, CHUNKS // 2, tell, 0)

        arrived(mom_rcv, MOM)

        def expand(b, carry):
            mu = mom_rcv[b].astype(F32)
            total = psi[0] * mu[0:1, :]
            for k in range(1, NODES):
                total = total + psi[k] * mu[k : k + 1, :]
            ebuf[b] = total
            return carry

        lax.fori_loop(0, CHUNKS, expand, 0)

        @pl.when(core == 1)
        def _():
            push_to(ebuf, sib_rcv, SIB, me - 1).start()

        far = jnp.exp(decay * float(-SPAN))

        def step(i, state):
            b = chunk_at(i)
            before[b] = state
            total = push[0] * state[0:1, :]
            for m in range(1, MODES):
                total = total + push[m] * state[m : m + 1, :]
            ent_send[b] = total.astype(BF16)
            send(ent_send.at[b], ent_rcv.at[core, block], ENT, b)
            return state * far + ebuf[b]

        lax.fori_loop(0, CHUNKS, step, jnp.zeros((MODES, SPAN), F32))

        @pl.when(core == 0)
        def _():
            arrived(sib_rcv, SIB)
            arrived(inn_rcv, INN)

            def cross(b, carry):
                total, inner = carry
                return total + before[b] * sib_rcv[b], inner + inn_rcv[b].astype(F32)

            zero = jnp.zeros((MODES, SPAN), F32)
            total, inner = lax.fori_loop(0, CHUNKS, cross, (zero, zero))
            total = total * keep
            for k in range(NODES):
                total = total + psi[k] * inner[k : k + 1, :]
            sco_send[...] = total * scale * (1.0 / math.sqrt(SPAN * CHUNKS))
            for k in range(8):
                send(sco_send, sco_rcv, SCO, 8 * block + k)

    arrived(kap_rcv, KAP)

    def gather(b, carry):
        cols = pl.ds(pl.multiple_of(b * SPAN, SPAN), SPAN)
        kappa = kap_rcv[b]
        for c, acc in ((0, y_acc), (1, r_acc)):
            total = prod[c, :SPAN, cols] * kappa[0:1, :]
            for k in range(1, NODES):
                total = total + prod[c, k * SPAN : (k + 1) * SPAN, cols] * kappa[k : k + 1, :]
            acc[:, cols] = total
        return carry

    lax.fori_loop(0, BLOCKS, gather, 0)
    arrived(ent_rcv, ENT)
    for b in range(BLOCKS):
        cols = slice(b * SPAN, (b + 1) * SPAN)
        for c, acc, out in ((0, y_acc, y_out), (1, r_acc, r_out)):
            entering = ent_rcv[c, b]
            both = jnp.concatenate([entering, entering], axis=0)
            total = acc[:, cols] + jnp.dot(spr[c], both, preferred_element_type=F32)
            out[:, cols] = total.astype(BF16)

    arrived(sco_rcv, SCO)
    s_out[...] = pltpu.roll(sco_rcv[...], lax.rem(SPAN - 16 * own_part, SPAN), 1)

    for args in moment_args + inner_args + param_args:
        sent(*args)

    @pl.when(scans)
    def _():
        def told(n, carry):
            sent(kap_send, kap_rcv.at[block], KAP, 2 * n + core)
            return carry

        lax.fori_loop(0, CHUNKS // 2, told, 0)

        def stepped(b, carry):
            sent(ent_send.at[b], ent_rcv.at[core, block], ENT, b)
            return carry

        lax.fori_loop(0, CHUNKS, stepped, 0)

        @pl.when(core == 1)
        def _():
            push_to(ebuf, sib_rcv, SIB, me - 1).wait_send()

        @pl.when(core == 0)
        def _():
            for k in range(8):
                sent(sco_send, sco_rcv, SCO, 8 * block + k)


def gated(left, right):
    return (left.astype(F32) * right.astype(F32)).astype(BF16)


def body(query_gate, key_gate, value_input, grad_out, residues, decay):
    toeplitz, moments, spread = (jnp.asarray(t) for t in tables())
    tokens, channels = query_gate.shape
    vm = pltpu.VMEM
    gate = vm((tokens, channels), BF16)
    scratch = [
        gate, gate, gate, gate, vm((OWN, MODES), F32), vm((OWN, MODES), F32),
        vm(toeplitz.shape, BF16), vm(moments.shape, BF16), vm(spread.shape, BF16),
        vm((2 * tokens, channels), BF16), vm((2 * tokens, channels), BF16),
        vm((2, NODES * SPAN, channels), F32), vm((NODES, channels), F32),
        vm((tokens, channels), F32), vm((tokens, channels), F32),
        vm((2, BLOCKS, NODES, SPAN), BF16), vm((BLOCKS, NODES, SPAN), BF16), vm((4, SPAN), F32),
        vm((CHUNKS, NODES, SPAN), BF16), vm((CHUNKS, NODES, SPAN), BF16), vm((8, 4, SPAN), F32),
        vm((BLOCKS, NODES, SPAN), F32), vm((2, BLOCKS, NODES, SPAN), BF16), vm((MODES, SPAN), F32),
        vm((CHUNKS, MODES, SPAN), F32),
        vm((NODES, MODES, SPAN), F32), vm((MODES, NODES, SPAN), F32), vm((CHUNKS, MODES, SPAN), F32),
        vm((CHUNKS, MODES, SPAN), F32), vm((CHUNKS, NODES, SPAN), BF16), vm((NODES, SPAN), F32),
        vm((MODES, SPAN), F32),
        pltpu.SemaphoreType.DMA((9,)), pltpu.SemaphoreType.DMA((7,)), pltpu.SemaphoreType.DMA((7,)),
    ]
    anywhere = pl.BlockSpec(memory_space=pl.ANY)
    vmem = pl.BlockSpec(memory_space=pltpu.VMEM)
    output, backward, score = pl.pallas_call(
        kernel,
        out_shape=(
            jax.ShapeDtypeStruct((tokens, channels), BF16),
            jax.ShapeDtypeStruct((tokens, channels), BF16),
            jax.ShapeDtypeStruct((MODES, SPAN), F32),
        ),
        in_specs=[anywhere] * 9,
        out_specs=(vmem, vmem, vmem),
        scratch_shapes=scratch,
        compiler_params=pltpu.CompilerParams(
            collective_id=0, has_side_effects=True, vmem_limit_bytes=50 * 2**20
        ),
        cost_estimate=pl.CostEstimate(flops=2**31, bytes_accessed=2**22, transcendentals=0),
        name="chunk_convolution",
    )(query_gate, key_gate, value_input, grad_out, residues, decay, toeplitz, moments, spread)
    return (
        gated(grad_out, output),
        gated(backward, value_input),
        gated(backward, key_gate),
        score[:, :OWN].T,
    )


def solution(mesh):
    gate = P("seq", "chan")
    rows = P(("chan", "seq"), None)
    return jax.shard_map(
        body,
        mesh=mesh,
        in_specs=(gate, gate, gate, gate, rows, rows),
        out_specs=(gate, gate, gate, rows),
        check_vma=False,
    )
```

time: 320 us -> 61.5 us (0.19)
  waiting for transfers between devices: 130 us -> 0 us
  local copies, waits for them, and re-layouts: 105 us -> 9.01 us
  starting transfers between devices: 56 us -> 0 us
  Pallas kernels: 0 us -> 50.3 us
  other arithmetic: 17.7 us -> 1.06 us
  matrix products: 7.92 us -> 0 us
    all_to_all x7 -> x0, waiting for transfers between devices: 130 us -> none  [the longest x1 22.9 us: body(): lax.all_to_all(gated(backward_b, moved_value), 'seq', split_axis=0, conca...]
    all_to_all x7 -> x0, starting transfers between devices: 56 us -> none  [the longest x1 19.8 us: body(): lax.all_to_all(query_gate, 'seq', split_axis=1, concat_axis=0, tiled=True)]
    pallas_call x0 -> x1, Pallas kernels: none -> 50.3 us  [body(): pl.pallas_call(kernel, out_shape=(jax.ShapeDtypeStruct((tokens, channels)...]
    slice x54 -> x0, local copies, waits for them, and re-layouts: 43.8 us -> none  [the longest x31 22.3 us: prepare(): lax.associative_scan(link, (step, starts), reverse=True, axis=0)[1]]
    pad x18 -> x0, local copies, waits for them, and re-layouts: 26.6 us -> none  [the longest x8 15.6 us: prepare(): lax.associative_scan(link, (step, starts), reverse=True, axis=0)[1]]
    add x29 -> x0, other arithmetic: 9.83 us -> none  [the longest x17 8.13 us: link(): return (earlier[0] * later[0], later[0] * earlier[1] + later[1])]
    unnamed x74 -> x25, local copies, waits for them, and re-layouts: 18.2 us -> 9.01 us
    reshape x2 -> x0, local copies, waits for them, and re-layouts: 8.42 us -> none  [the longest x1 4.8 us: toeplitz(): return flat.reshape(channels, blk, 2 * blk - 2)[:, :, :blk]]
  transfers between devices with their start and end apart: 7 -> 0, of which waited for: 6 -> 0; matrix products, arithmetic and copies ran while one was open for 15% -> 0% of each run, Pallas kernels for 0% -> 0%
where the time goes in v1:
time: 61.5 us; the launch traced here: 61.1 us
  Pallas kernels  50.3 us (82%)
  local copies, waits for them, and re-layouts  9.01 us (15%)
  other arithmetic  1.06 us (2%)
  between operations  0.67 us (1%)
    pallas_call x1, Pallas kernels, body(): pl.pallas_call(kernel, out_shape=(jax.ShapeDtypeStruct((tokens, channels)...  50.3 us
    unnamed x25, local copies, waits for them, and re-layouts  9.01 us

profile of v1, /device:TPU:1, one launch (start us, length us, event | category | flops | bytes accessed | tf_op | source)
XLA Modules:
  0.0 61.1 jit_solution(12828293060960713855)
XLA Ops:
  0.6 0.0 copy-start
  0.6 0.9 %copy-done = bf16[128,1024]{1,0:T(8,128)(2,1)S(1)} copy-done((bf16[128,1024]{1,0:T(8,128)(2,1)S(1)}, bf16[128,1024]{1,0:T(8,128)(2,1)}, u32[]{:S(2)}) %copy-start) | copy-done | bytes 262168
  1.6 0.0 copy-start.2
  1.6 0.9 %copy-done.2 = bf16[128,1024]{1,0:T(8,128)(2,1)S(1)} copy-done((bf16[128,1024]{1,0:T(8,128)(2,1)S(1)}, bf16[128,1024]{1,0:T(8,128)(2,1)}, u32[]{:S(2)}) %copy-start.2) | copy-done | bytes 262168
  2.5 0.0 copy-start.4
  2.5 0.9 %copy-done.4 = bf16[128,1024]{1,0:T(8,128)(2,1)S(1)} copy-done((bf16[128,1024]{1,0:T(8,128)(2,1)S(1)}, bf16[128,1024]{1,0:T(8,128)(2,1)}, u32[]{:S(2)}) %copy-start.4) | copy-done | bytes 262168
  3.5 0.9 %copy-done.6 = bf16[128,1024]{1,0:T(8,128)(2,1)S(1)} copy-done((bf16[128,1024]{1,0:T(8,128)(2,1)S(1)}, bf16[128,1024]{1,0:T(8,128)(2,1)}, u32[]{:S(2)}) %copy-start.6) | copy-done | bytes 262168
  4.4 0.0 copy-start.7
  4.4 0.7 %copy-done.7 = f32[16,16]{1,0:T(8,128)S(1)} copy-done((f32[16,16]{1,0:T(8,128)S(1)}, f32[16,16]{1,0:T(8,128)}, u32[]{:S(2)}) %copy-start.7) | copy-done | bytes 1048
  5.1 0.0 copy-start.8
  5.1 0.7 %copy-done.8 = f32[16,16]{1,0:T(8,128)S(1)} copy-done((f32[16,16]{1,0:T(8,128)S(1)}, f32[16,16]{1,0:T(8,128)}, u32[]{:S(2)}) %copy-start.8) | copy-done | bytes 1048
  5.8 0.0 copy-start.9
  5.8 1.6 %copy-done.9 = bf16[2,2048,256]{2,1,0:T(8,128)(2,1)S(1)} copy-done((bf16[2,2048,256]{2,1,0:T(8,128)(2,1)S(1)}, bf16[2,2048,256]{2,1,0:T(8,128)(2,1)}, u32[]{:S(2)}) %copy-start.9) | copy-done | bytes 2097176
  7.4 0.0 copy-start.10
  7.4 0.8 %copy-done.10 = bf16[2,128,32]{2,1,0:T(8,128)(2,1)S(1)} copy-done((bf16[2,128,32]{2,1,0:T(8,128)(2,1)S(1)}, bf16[2,128,32]{2,1,0:T(8,128)(2,1)}, u32[]{:S(2)}) %copy-start.10) | copy-done | bytes 16408
  8.3 0.0 copy-start.11
  8.3 0.7 %copy-done.11 = bf16[2,16,256]{2,1,0:T(8,128)(2,1)S(1)} copy-done((bf16[2,16,256]{2,1,0:T(8,128)(2,1)S(1)}, bf16[2,16,256]{2,1,0:T(8,128)(2,1)}, u32[]{:S(2)}) %copy-start.11) | copy-done | bytes 16408
  9.0 0.0 copy-start.1
  9.0 50.3 %chunk_convolution.1 = (bf16[128,1024]{1,0:T(8,128)(2,1)S(1)}, bf16[128,1024]{1,0:T(8,128)(2,1)S(1)}, f32[16,128]{1,0:T(8,128)S(1)}) custom-call(bf16[128,1024]{1,0:T(8,128)(2,1)S(1)} %copy-done.6, bf16[128,1024]{1,0:T(8,128)(2,1)S(1)} %copy-done, bf16[128,1024]{1,0:T(8,128)(2,1)S(1)} %copy-done.2, bf16[128,1024]{1,0:T(8,128)(2,1)S(1)} %copy-done.4, ...), custom_call_target="tpu_custom_call" | custom-call | flops 2147483648 | bytes 4194304 | tf_op jit(solution)/shard_map/chunk_convolution/pallas_call | solution.py:387
  59.3 0.7 %copy.13 = f32[16,16]{1,0:T(8,128)} copy(f32[16,16]{0,1:T(8,128)S(1)} %slice_bitcast_fusion) | data formatting | bytes 2048
  60.0 0.0 copy-done.1
  60.0 0.0 copy-done.3
  60.0 0.0 copy-done.5
  60.0 1.1 %fusion.1 = (bf16[128,1024]{1,0:T(8,128)(2,1)}, bf16[128,1024]{1,0:T(8,128)(2,1)}, bf16[128,1024]{1,0:T(8,128)(2,1)}) fusion(bf16[128,1024]{1,0:T(8,128)(2,1)S(1)} %get-tuple-element.8, bf16[128,1024]{1,0:T(8,128)(2,1)S(1)} %copy-done.1, bf16[128,1024]{1,0:T(8,128)(2,1)S(1)} %copy-done.3, bf16[128,1024]{1,0:T(8,128)(2,1)S(1)} %get-tuple-element.7, ...), kind=kLoop, calls=%fused_computation.3 | loop fusion | flops 1441792 | bytes 2097152 | tf_op jit(solution)/shard_map/convert_element_type | solution.py:362
  (4 shorter events, 0.0 us)
Async XLA Ops:
  0.6 1.0 %copy-start = (bf16[128,1024]{1,0:T(8,128)(2,1)S(1)}, bf16[128,1024]{1,0:T(8,128)(2,1)}, u32[]{:S(2)}) copy-start(bf16[128,1024]{1,0:T(8,128)(2,1)} %k_hbm.1) | copy-start | bytes 786436
  1.6 0.9 %copy-start.2 = (bf16[128,1024]{1,0:T(8,128)(2,1)S(1)}, bf16[128,1024]{1,0:T(8,128)(2,1)}, u32[]{:S(2)}) copy-start(bf16[128,1024]{1,0:T(8,128)(2,1)} %v_hbm.1) | copy-start | bytes 786436
  2.5 0.9 %copy-start.4 = (bf16[128,1024]{1,0:T(8,128)(2,1)S(1)}, bf16[128,1024]{1,0:T(8,128)(2,1)}, u32[]{:S(2)}) copy-start(bf16[128,1024]{1,0:T(8,128)(2,1)} %go_hbm.1) | copy-start | bytes 786436
  3.5 0.9 %copy-start.6 = (bf16[128,1024]{1,0:T(8,128)(2,1)S(1)}, bf16[128,1024]{1,0:T(8,128)(2,1)}, u32[]{:S(2)}) copy-start(bf16[128,1024]{1,0:T(8,128)(2,1)} %q_hbm.1) | copy-start | bytes 786436
  4.4 0.7 %copy-start.7 = (f32[16,16]{1,0:T(8,128)S(1)}, f32[16,16]{1,0:T(8,128)}, u32[]{:S(2)}) copy-start(f32[16,16]{1,0:T(8,128)} %res_hbm.1) | copy-start | bytes 3076
  5.1 0.7 %copy-start.8 = (f32[16,16]{1,0:T(8,128)S(1)}, f32[16,16]{1,0:T(8,128)}, u32[]{:S(2)}) copy-start(f32[16,16]{1,0:T(8,128)} %dec_hbm.1) | copy-start | bytes 3076
  5.8 1.6 %copy-start.9 = (bf16[2,2048,256]{2,1,0:T(8,128)(2,1)S(1)}, bf16[2,2048,256]{2,1,0:T(8,128)(2,1)}, u32[]{:S(2)}) copy-start(bf16[2,2048,256]{2,1,0:T(8,128)(2,1)} %constant.6.clone.toe_hbm) | copy-start | bytes 6291460
  7.4 0.8 %copy-start.10 = (bf16[2,128,32]{2,1,0:T(8,128)(2,1)S(1)}, bf16[2,128,32]{2,1,0:T(8,128)(2,1)}, u32[]{:S(2)}) copy-start(bf16[2,128,32]{2,1,0:T(8,128)(2,1)} %constant.8.clone.spr_hbm) | copy-start | bytes 49156
  8.3 0.7 %copy-start.11 = (bf16[2,16,256]{2,1,0:T(8,128)(2,1)S(1)}, bf16[2,16,256]{2,1,0:T(8,128)(2,1)}, u32[]{:S(2)}) copy-start(bf16[2,16,256]{2,1,0:T(8,128)(2,1)} %constant.7.clone.mom_hbm) | copy-start | bytes 49156
  9.0 51.0 %copy-start.1 = (bf16[128,1024]{1,0:T(8,128)(2,1)S(1)}, bf16[128,1024]{1,0:T(8,128)(2,1)}, u32[]{:S(2)}) copy-start(bf16[128,1024]{1,0:T(8,128)(2,1)} %k_hbm.1) | copy-start | bytes 786436
  9.0 51.0 %copy-start.3 = (bf16[128,1024]{1,0:T(8,128)(2,1)S(1)}, bf16[128,1024]{1,0:T(8,128)(2,1)}, u32[]{:S(2)}) copy-start(bf16[128,1024]{1,0:T(8,128)(2,1)} %v_hbm.1) | copy-start | bytes 786436
  9.0 51.0 %copy-start.5 = (bf16[128,1024]{1,0:T(8,128)(2,1)S(1)}, bf16[128,1024]{1,0:T(8,128)(2,1)}, u32[]{:S(2)}) copy-start(bf16[128,1024]{1,0:T(8,128)(2,1)} %go_hbm.1) | copy-start | bytes 786436

commit v2 on v1

v2 whole, which is shorter than its diff:
```python
import functools
import math

import jax
import jax.numpy as jnp
import ml_dtypes
import numpy as np
from jax import lax
from jax.experimental import pallas as pl
from jax.experimental.pallas import tpu as pltpu
from jax.sharding import PartitionSpec as P

MESH = pl.DeviceIdType.MESH
F32 = jnp.float32
BF16 = jnp.bfloat16
SPAN = 128
PAIR = 2 * SPAN
NODES = 16
MODES = 16
BLOCKS = 8
DEVICES = 64
CHUNKS = 32
OWN = 16
BEND = 200.0
Z_FIRST, Z_STEP = 0, 1
NEAR = 4
MOM, INN, PRM, KAP, ENT, SCO, SIB, PART, SEQ, RLY = range(10)


def scan_device(block, core):
    z = (Z_FIRST + Z_STEP * (block % 4)) % 16
    return (block // 4) * 32 + z * 2 + core


def bent(lag):
    return lag / (lag + BEND)


def bent_nodes():
    k = np.arange(NODES)
    half = bent(PAIR - 1.0) / 2.0
    return half + half * np.cos(np.pi * (2 * k + 1) / (2 * NODES))


def nodes():
    u = bent_nodes()
    return BEND * u / (1.0 - u)


def cardinal():
    u = bent_nodes()
    at = bent(np.arange(PAIR, dtype=np.float64))
    out = np.ones((NODES, PAIR))
    for k in range(NODES):
        for j in range(NODES):
            if j != k:
                out[k] *= (at - u[j]) / (u[k] - u[j])
    return out


def split(a, axis):
    high = a.astype(ml_dtypes.bfloat16)
    low = (a - high.astype(np.float64)).astype(ml_dtypes.bfloat16)
    return np.concatenate([high, low], axis=axis)


@functools.cache
def tables():
    phi = cardinal()
    t = np.arange(SPAN)
    lag = t[:, None] - t[None, :]
    inside = lag >= 0
    own = np.where(inside[None], phi[:, np.where(inside, lag, 0)], 0.0)
    cross = phi[:, lag + SPAN]
    toeplitz = np.stack([np.concatenate([a, b], axis=-1) for a, b in (
        (own, cross), (own.transpose(0, 2, 1), cross.transpose(0, 2, 1)))])
    toeplitz = toeplitz.reshape(2, NODES * SPAN, PAIR).astype(ml_dtypes.bfloat16)
    ahead, behind = phi[:, :SPAN], phi[:, SPAN:]
    moments = np.stack([np.stack([split(a, 0) for a in pair]) for pair in (
        (behind[:, ::-1], ahead), (ahead[:, ::-1], behind))])
    spread = np.stack([np.stack([split(a.T, 1) for a in pair]) for pair in (
        (ahead, behind[:, ::-1]), (behind, ahead[:, ::-1]))])
    return toeplitz, moments.reshape(4, 2 * NODES, SPAN), spread.reshape(4, SPAN, 2 * NODES)


def falling(u):
    total = jnp.full_like(u, -1.0 / 5040.0)
    for c in (720.0, -120.0, 24.0, -6.0, 2.0, -1.0):
        total = total * u - 1.0 / c
    return total * u


def kernel(
    q_hbm, k_hbm, v_hbm, go_hbm, res_hbm, dec_hbm, toe_hbm, mom_hbm, spr_hbm,
    y_out, r_out, s_out,
    q_in, k_in, v_in, go_in, res_in, dec_in, toe, mom, spr,
    x2, g2, prod, inn, y_acc, r_acc,
    part_send, part_rcv,
    mom_send, inn_send, prm_send,
    mom_rcv, inn_rcv, prm_rcv, kap_rcv, ent_rcv, sco_rcv, sib_rcv,
    psi, push, ebuf, before, ent_send, kap_send, sco_send, scalers,
    in_sem, send_sem, recv_sem,
):
    me = lax.axis_index("seq")
    core = lax.rem(me, 2)
    chip = lax.div(me, 2)
    sibling = me + 1 - 2 * core
    z = lax.rem(chip, 16)
    y_hi = lax.div(me, 32)
    ahead = lax.rem(z - Z_FIRST + 16, 16)
    scans = jnp.logical_and(lax.rem(ahead, Z_STEP) == 0, ahead < 4 * Z_STEP)
    block = y_hi * 4 + lax.rem(lax.div(ahead, Z_STEP), 4)
    own_block, own_part = lax.div(me, 8), lax.rem(me, 8)

    def scanner_of(b, c):
        return lax.div(b, 4) * 32 + lax.rem(Z_FIRST + Z_STEP * lax.rem(b, 4), 16) * 2 + c

    loads = [
        pltpu.make_async_copy(src, dst, in_sem.at[n])
        for n, (src, dst) in enumerate(
            [
                (res_hbm, res_in), (dec_hbm, dec_in),
                (k_hbm, k_in), (v_hbm, v_in), (go_hbm, go_in), (q_hbm, q_in), (mom_hbm, mom), (spr_hbm, spr), (toe_hbm, toe),
            ]
        )
    ]
    for load in loads:
        load.start()

    barrier = pltpu.get_barrier_semaphore()

    def greet(device):
        pl.semaphore_signal(barrier, inc=1, device_id={"seq": device}, device_id_type=MESH)

    @pl.when(scans)
    def _():
        def one(n, carry):
            greet(lax.rem(me + n, DEVICES))
            return carry

        lax.fori_loop(1, DEVICES, one, 0)

    @pl.when(jnp.logical_not(scans))
    def _():
        greet(sibling)
        for b in range(BLOCKS):
            for c in range(2):
                greet(scan_device(b, c))

    def push_to(src, dst, kind, device):
        return pltpu.make_async_remote_copy(
            src_ref=src, dst_ref=dst, send_sem=send_sem.at[kind], recv_sem=recv_sem.at[kind],
            device_id={"seq": device}, device_id_type=MESH,
        )

    def send(src, dst, kind, device):
        @pl.when(me != device)
        def _():
            push_to(src, dst, kind, device).start()

        @pl.when(me == device)
        def _():
            pltpu.make_async_copy(src, dst, recv_sem.at[kind]).start()

    def sent(src, dst, kind, device):
        @pl.when(me != device)
        def _():
            push_to(src, dst, kind, device).wait_send()

    def arrived(ref, kind):
        pltpu.make_async_copy(ref, ref, recv_sem.at[kind]).wait()

    loads[0].wait()
    loads[1].wait()
    lane16 = lax.broadcasted_iota(jnp.int32, (OWN, SPAN), 1)
    row16 = lax.broadcasted_iota(jnp.int32, (OWN, SPAN), 0)
    for n, ref in ((0, dec_in), (1, res_in)):
        value = ref[...]
        for r in range(2):
            wide = jnp.zeros((OWN, SPAN), F32)
            for j in range(8):
                column = jnp.broadcast_to(value[:, 8 * r + j : 8 * r + j + 1], (OWN, SPAN))
                wide = jnp.where(lane16 // 16 == j, column, wide)
            wide = jnp.where(lane16 % 16 == row16, wide, 0.0)
            prm_send[2 * n + r : 2 * n + r + 1, :] = jnp.sum(wide, axis=0, keepdims=True)

    for n in (2, 3, 4, 5, 6):
        loads[n].wait()
    x = (k_in[...].astype(F32) * v_in[...].astype(F32)).astype(BF16)
    g = (go_in[...].astype(F32) * q_in[...].astype(F32)).astype(BF16)
    x2[:SPAN, :] = x
    g2[:SPAN, :] = g

    def moment(c, value):
        both = jnp.dot(mom[2 * core + c], value, preferred_element_type=F32)
        return both[:NODES] + both[NODES:]

    of_x, of_g = moment(0, x), moment(1, g)
    first = core == 0
    part_send[...] = jnp.where(first, of_g, of_x)
    kept = jnp.where(first, of_x, of_g)

    @pl.when(scans)
    def _():
        pl.semaphore_wait(barrier, DEVICES - 1)

    @pl.when(jnp.logical_not(scans))
    def _():
        pl.semaphore_wait(barrier, 2 * BLOCKS + 1)

    param_args = [(prm_send, prm_rcv.at[own_part], PRM, scanner_of(own_block, c)) for c in range(2)]
    for args in param_args:
        send(*args)

    part = push_to(part_send, part_rcv, PART, sibling)
    part.start()

    @pl.when(first)
    def _():
        push_to(x2.at[pl.ds(0, SPAN)], x2.at[pl.ds(SPAN, SPAN)], SEQ, sibling).start()
        x2[SPAN:, :] = jnp.zeros((SPAN, x2.shape[1]), BF16)

    @pl.when(jnp.logical_not(first))
    def _():
        push_to(g2.at[pl.ds(0, SPAN)], g2.at[pl.ds(SPAN, SPAN)], SEQ, sibling).start()
        g2[SPAN:, :] = jnp.zeros((SPAN, g2.shape[1]), BF16)

    arrived(part_rcv, PART)
    total = (kept + part_rcv[...]).astype(BF16)
    for b in range(BLOCKS):
        mom_send[b] = total[:, b * SPAN : (b + 1) * SPAN]
    moment_args = [(mom_send.at[b], mom_rcv.at[chip], MOM, scan_device(b, 0) + core) for b in range(BLOCKS)]
    for args in moment_args:
        send(*args)

    loads[7].wait()
    loads[8].wait()

    @pl.when(first)
    def _():
        arrived(g2.at[pl.ds(SPAN, SPAN)], SEQ)

    @pl.when(jnp.logical_not(first))
    def _():
        arrived(x2.at[pl.ds(SPAN, SPAN)], SEQ)

    def onward(j, carry):
        cols = pl.ds(pl.multiple_of(j * 256, 256), 256)
        prod[0, :, cols] = jnp.dot(toe[0], x2[:, cols], preferred_element_type=F32)
        grad = g2[:SPAN, cols].astype(F32)
        for k in range(NODES):
            inn[k : k + 1, cols] = jnp.sum(
                prod[0, k * SPAN : (k + 1) * SPAN, cols] * grad, axis=0, keepdims=True
            )
        return carry

    lax.fori_loop(0, 4, onward, 0)
    for b in range(BLOCKS):
        inn_send[b] = inn[:, b * SPAN : (b + 1) * SPAN].astype(BF16)
    inner_args = [(inn_send.at[b], inn_rcv.at[me], INN, scan_device(b, 0)) for b in range(BLOCKS)]
    for args in inner_args:
        send(*args)

    def back(j, carry):
        cols = pl.ds(pl.multiple_of(j * 256, 256), 256)
        prod[1, :, cols] = jnp.dot(toe[1], g2[:, cols], preferred_element_type=F32)
        return carry

    lax.fori_loop(0, 4, back, 0)

    def chunk_at(i):
        return i + core * (CHUNKS - 1 - 2 * i)

    def by_z(n):
        return lax.rem(n, 2) * 16 + lax.div(n, 2)

    @pl.when(scans)
    def _():
        arrived(prm_rcv, PRM)
        lane8 = lax.broadcasted_iota(jnp.int32, (8, SPAN), 1)
        row8 = lax.broadcasted_iota(jnp.int32, (8, SPAN), 0)
        halves = []
        for r in range(4):
            packed = jnp.concatenate([prm_rcv[k, r : r + 1, :] for k in range(8)], axis=0)
            skewed = pltpu.roll(packed, 0, 1, stride=16, stride_axis=0)
            out = jnp.zeros((8, SPAN), F32)
            for j in range(8):
                turned = pltpu.roll(skewed, (SPAN - 16 * j) % SPAN, 1)
                turned = jnp.where(lane8 // 16 == row8, turned, 0.0)
                out = jnp.where(row8 == j, jnp.sum(turned, axis=0, keepdims=True), out)
            halves.append(out)
        decay = jnp.concatenate(halves[:2], axis=0)
        residue = jnp.concatenate(halves[2:], axis=0)
        scale = jnp.sqrt(falling(2.0 * decay))
        gain = residue * scale
        keep = 1.0 - falling(decay)
        points = nodes()
        for k in range(NODES):
            psi[k] = jnp.exp(decay * float(-points[k]))
        where = jnp.zeros((NODES, SPAN), F32)
        rows = lax.broadcasted_iota(jnp.int32, (NODES, SPAN), 0)
        for k in range(NODES):
            where = jnp.where(rows == k, float(-points[k]), where)
        kappa = jnp.zeros((NODES, SPAN), F32)
        for m in range(MODES):
            wave = jnp.exp(where * decay[m : m + 1, :]) * gain[m : m + 1, :]
            kappa = kappa + wave
            push[m] = wave * keep[m : m + 1, :]
        kap_send[...] = kappa.astype(BF16)
        scalers[0], scalers[1] = scale, keep

        def tell(n, carry):
            @pl.when(jnp.logical_or(lax.div(n, 2) < NEAR, lax.rem(lax.div(n, 2), 2) == core))
            def _():
                send(kap_send, kap_rcv.at[block], KAP, 2 * by_z(n) + core)

            return carry

        lax.fori_loop(0, CHUNKS, tell, 0)

        arrived(mom_rcv, MOM)

        def expand(b, carry):
            mu = mom_rcv[b].astype(F32)
            total = psi[0] * mu[0:1, :]
            for k in range(1, NODES):
                total = total + psi[k] * mu[k : k + 1, :]
            ebuf[b] = total
            return carry

        lax.fori_loop(0, CHUNKS, expand, 0)

        @pl.when(core == 1)
        def _():
            push_to(ebuf, sib_rcv, SIB, me - 1).start()

        far = jnp.exp(decay * float(-PAIR))

        def step(i, state):
            b = chunk_at(i)
            before[b] = state
            total = push[0] * state[0:1, :]
            for m in range(1, MODES):
                total = total + push[m] * state[m : m + 1, :]
            ent_send[b] = total.astype(BF16)
            return state * far + ebuf[b]

        lax.fori_loop(0, CHUNKS, step, jnp.zeros((MODES, SPAN), F32))

        def tell_entering(n, carry):
            b = by_z(n)
            send(ent_send.at[b], ent_rcv.at[core, block], ENT, 2 * b + core)

            @pl.when(lax.div(n, 2) < NEAR)
            def _():
                send(ent_send.at[b], ent_rcv.at[core, block], ENT, 2 * b + 1 - core)

            return carry

        lax.fori_loop(0, CHUNKS, tell_entering, 0)

    arrived(kap_rcv, KAP)
    passes_taps = jnp.logical_and(z >= NEAR, lax.rem(z, 2) == core)

    @pl.when(passes_taps)
    def _():
        push_to(kap_rcv, kap_rcv, KAP, sibling).start()

    def gather(b, carry):
        cols = pl.ds(pl.multiple_of(b * SPAN, SPAN), SPAN)
        kappa = kap_rcv[b].astype(F32)
        for c, acc in ((0, y_acc), (1, r_acc)):
            total = prod[c, :SPAN, cols] * kappa[0:1, :]
            for k in range(1, NODES):
                total = total + prod[c, k * SPAN : (k + 1) * SPAN, cols] * kappa[k : k + 1, :]
            acc[:, cols] = total
        return carry

    lax.fori_loop(0, BLOCKS, gather, 0)
    @pl.when(jnp.logical_and(scans, first))
    def _():
        scale, keep = scalers[0], scalers[1]
        arrived(sib_rcv, SIB)
        arrived(inn_rcv, INN)

        def cross(b, carry):
            total, inner = carry
            both = inn_rcv[2 * b].astype(F32) + inn_rcv[2 * b + 1].astype(F32)
            return total + before[b] * sib_rcv[b], inner + both

        zero = jnp.zeros((MODES, SPAN), F32)
        total, inner = lax.fori_loop(0, CHUNKS, cross, (zero, zero))
        total = total * keep
        for k in range(NODES):
            total = total + psi[k] * inner[k : k + 1, :]
        sco_send[...] = total * scale * (1.0 / math.sqrt(SPAN * DEVICES))
        for k in range(8):
            send(sco_send, sco_rcv, SCO, 8 * block + k)

    near = z < NEAR

    @pl.when(near)
    def _():
        arrived(ent_rcv, ENT)

    def relay():
        return push_to(ent_rcv.at[core], ent_rcv.at[core], RLY, sibling)

    @pl.when(jnp.logical_not(near))
    def _():
        arrived(ent_rcv.at[core], ENT)
        relay().start()
        arrived(ent_rcv.at[1 - core], RLY)

    for b in range(BLOCKS):
        cols = slice(b * SPAN, (b + 1) * SPAN)
        for c, acc, out in ((0, y_acc, y_out), (1, r_acc, r_out)):
            entering = ent_rcv[c, b]
            both = jnp.concatenate([entering, entering], axis=0)
            total = acc[:, cols] + jnp.dot(spr[2 * core + c], both, preferred_element_type=F32)
            out[:, cols] = total.astype(BF16)

    arrived(sco_rcv, SCO)
    turned = pltpu.roll(sco_rcv[...], lax.rem(SPAN - 16 * own_part, SPAN), 1)
    s_out[...] = jnp.transpose(turned)[:OWN, :]

    for args in moment_args + inner_args + param_args:
        sent(*args)
    part.wait_send()

    @pl.when(z >= NEAR)
    def _():
        relay().wait_send()

    @pl.when(passes_taps)
    def _():
        push_to(kap_rcv, kap_rcv, KAP, sibling).wait_send()

    @pl.when(first)
    def _():
        push_to(x2.at[pl.ds(0, SPAN)], x2.at[pl.ds(SPAN, SPAN)], SEQ, sibling).wait_send()

    @pl.when(jnp.logical_not(first))
    def _():
        push_to(g2.at[pl.ds(0, SPAN)], g2.at[pl.ds(SPAN, SPAN)], SEQ, sibling).wait_send()

    @pl.when(scans)
    def _():
        def told(n, carry):
            @pl.when(jnp.logical_or(lax.div(n, 2) < NEAR, lax.rem(lax.div(n, 2), 2) == core))
            def _():
                sent(kap_send, kap_rcv.at[block], KAP, 2 * by_z(n) + core)

            return carry

        lax.fori_loop(0, CHUNKS, told, 0)

        def stepped(n, carry):
            b = by_z(n)
            sent(ent_send.at[b], ent_rcv.at[core, block], ENT, 2 * b + core)

            @pl.when(lax.div(n, 2) < NEAR)
            def _():
                sent(ent_send.at[b], ent_rcv.at[core, block], ENT, 2 * b + 1 - core)

            return carry

        lax.fori_loop(0, CHUNKS, stepped, 0)

        @pl.when(core == 1)
        def _():
            push_to(ebuf, sib_rcv, SIB, me - 1).wait_send()

        @pl.when(core == 0)
        def _():
            for k in range(8):
                sent(sco_send, sco_rcv, SCO, 8 * block + k)


def gated(left, right):
    return (left.astype(F32) * right.astype(F32)).astype(BF16)


def body(query_gate, key_gate, value_input, grad_out, residues, decay):
    toeplitz, moments, spread = (jnp.asarray(t) for t in tables())
    tokens, channels = query_gate.shape
    vm = pltpu.VMEM
    gate = vm((tokens, channels), BF16)
    scratch = [
        gate, gate, gate, gate, vm((OWN, MODES), F32), vm((OWN, MODES), F32),
        vm(toeplitz.shape, BF16), vm(moments.shape, BF16), vm(spread.shape, BF16),
        vm((PAIR, channels), BF16), vm((PAIR, channels), BF16),
        vm((2, NODES * SPAN, channels), F32), vm((NODES, channels), F32),
        vm((tokens, channels), F32), vm((tokens, channels), F32),
        vm((NODES, channels), F32), vm((NODES, channels), F32),
        vm((BLOCKS, NODES, SPAN), BF16), vm((BLOCKS, NODES, SPAN), BF16), vm((4, SPAN), F32),
        vm((CHUNKS, NODES, SPAN), BF16), vm((DEVICES, NODES, SPAN), BF16), vm((8, 4, SPAN), F32),
        vm((BLOCKS, NODES, SPAN), BF16), vm((2, BLOCKS, NODES, SPAN), BF16), vm((MODES, SPAN), F32),
        vm((CHUNKS, MODES, SPAN), F32),
        vm((NODES, MODES, SPAN), F32), vm((MODES, NODES, SPAN), F32), vm((CHUNKS, MODES, SPAN), F32),
        vm((CHUNKS, MODES, SPAN), F32), vm((CHUNKS, NODES, SPAN), BF16), vm((NODES, SPAN), BF16),
        vm((MODES, SPAN), F32), vm((2, MODES, SPAN), F32),
        pltpu.SemaphoreType.DMA((9,)), pltpu.SemaphoreType.DMA((10,)), pltpu.SemaphoreType.DMA((10,)),
    ]
    hbm = pl.BlockSpec(memory_space=pltpu.HBM)
    vmem = pl.BlockSpec(memory_space=pltpu.VMEM)
    output, backward, score = pl.pallas_call(
        kernel,
        out_shape=(
            jax.ShapeDtypeStruct((tokens, channels), BF16),
            jax.ShapeDtypeStruct((tokens, channels), BF16),
            jax.ShapeDtypeStruct((OWN, MODES), F32),
        ),
        in_specs=[hbm] * 9,
        out_specs=(vmem, vmem, vmem),
        scratch_shapes=scratch,
        compiler_params=pltpu.CompilerParams(
            collective_id=0, has_side_effects=True, vmem_limit_bytes=48 * 2**20
        ),
        cost_estimate=pl.CostEstimate(flops=2**31, bytes_accessed=2**22, transcendentals=0),
        name="chunk_convolution",
    )(*(pltpu.with_memory_space_constraint(a, pltpu.HBM) for a in (
        query_gate, key_gate, value_input, grad_out, residues, decay, toeplitz, moments, spread)))
    return (
        gated(grad_out, output),
        gated(backward, value_input),
        gated(backward, key_gate),
        score,
    )


def solution(mesh):
    gate = P("seq", "chan")
    rows = P(("chan", "seq"), None)
    return jax.shard_map(
        body,
        mesh=mesh,
        in_specs=(gate, gate, gate, gate, rows, rows),
        out_specs=(gate, gate, gate, rows),
        check_vma=False,
    )
```

time: 61.5 us -> 35.9 us (0.58)
  Pallas kernels: 50.3 us -> 33.4 us
  local copies, waits for them, and re-layouts: 9.01 us -> 0.61 us
    pallas_call x1, Pallas kernels: 50.3 us -> 33.4 us  [body(): pl.pallas_call(kernel, out_shape=(jax.ShapeDtypeStruct((tokens, channels)...]
    unnamed x25 -> x7, local copies, waits for them, and re-layouts: 9.01 us -> 0.61 us
where the time goes in v2:
time: 35.9 us; the launch traced here: 35.7 us
  Pallas kernels  33.4 us (93%)
  other arithmetic  1.06 us (3%)
  between operations  0.69 us (2%)
  local copies, waits for them, and re-layouts  0.61 us (2%)
    pallas_call x1, Pallas kernels, body(): pl.pallas_call(kernel, out_shape=(jax.ShapeDtypeStruct((tokens, channels)...  33.4 us
    convert_element_type x1, other arithmetic, gated(): return (left.astype(F32) * right.astype(F32)).astype(BF16)  1.06 us

profile of v2, /device:TPU:1, one launch (start us, length us, event | category | flops | bytes accessed | tf_op | source)
XLA Modules:
  0.0 35.7 jit_solution(14021153573429033945)
XLA Ops:
  0.6 0.0 copy-start.2
  0.6 0.0 copy-start.1
  0.7 0.0 copy-start
  0.7 33.4 %chunk_convolution.1 = (bf16[128,1024]{1,0:T(8,128)(2,1)S(1)}, bf16[128,1024]{1,0:T(8,128)(2,1)S(1)}, f32[16,16]{1,0:T(8,128)S(1)}) custom-call(bf16[128,1024]{1,0:T(8,128)(2,1)} %q_hbm.1, bf16[128,1024]{1,0:T(8,128)(2,1)} %k_hbm.1, bf16[128,1024]{1,0:T(8,128)(2,1)} %v_hbm.1, bf16[128,1024]{1,0:T(8,128)(2,1)} %go_hbm.1, f32[16,16]{1,0:T(8,128)} %res_hbm.1, ...), custom_call_target="tpu_custom_call" | custom-call | flops 2147483648 | bytes 4194304 | tf_op jit(solution)/shard_map/chunk_convolution/pallas_call | solution.py:507
  34.0 0.0 copy-done.2
  34.0 0.0 copy-done.1
  34.0 0.0 copy-done
  34.1 1.1 %fusion.1 = (bf16[128,1024]{1,0:T(8,128)(2,1)}, bf16[128,1024]{1,0:T(8,128)(2,1)}, bf16[128,1024]{1,0:T(8,128)(2,1)}) fusion(bf16[128,1024]{1,0:T(8,128)(2,1)S(1)} %get-tuple-element.8, bf16[128,1024]{1,0:T(8,128)(2,1)S(1)} %copy-done, bf16[128,1024]{1,0:T(8,128)(2,1)S(1)} %copy-done.1, bf16[128,1024]{1,0:T(8,128)(2,1)S(1)} %get-tuple-element.7, ...), kind=kLoop, calls=%fused_computation.3 | loop fusion | flops 1441792 | bytes 2097152 | tf_op jit(solution)/shard_map/convert_element_type | solution.py:481
  35.1 0.6 %copy.14 = f32[16,16]{1,0:T(8,128)} copy(f32[16,16]{1,0:T(8,128)S(1)} %get-tuple-element.20) | data formatting | bytes 2048
Async XLA Ops:
  0.6 33.4 %copy-start.2 = (bf16[128,1024]{1,0:T(8,128)(2,1)S(1)}, bf16[128,1024]{1,0:T(8,128)(2,1)}, u32[]{:S(2)}) copy-start(bf16[128,1024]{1,0:T(8,128)(2,1)} %go_hbm.1) | copy-start | bytes 786436
  0.6 33.4 %copy-start.1 = (bf16[128,1024]{1,0:T(8,128)(2,1)S(1)}, bf16[128,1024]{1,0:T(8,128)(2,1)}, u32[]{:S(2)}) copy-start(bf16[128,1024]{1,0:T(8,128)(2,1)} %v_hbm.1) | copy-start | bytes 786436
  0.7 33.4 %copy-start = (bf16[128,1024]{1,0:T(8,128)(2,1)S(1)}, bf16[128,1024]{1,0:T(8,128)(2,1)}, u32[]{:S(2)}) copy-start(bf16[128,1024]{1,0:T(8,128)(2,1)} %k_hbm.1) | copy-start | bytes 786436

commit v3 on v2

--- a/solution.py
+++ b/solution.py
@@ -24,7 +24,7 @@
 BEND = 200.0
 Z_FIRST, Z_STEP = 0, 1
 NEAR = 4
-MOM, INN, PRM, KAP, ENT, SCO, SIB, PART, SEQ, RLY = range(10)
+MOM, INN, PRM, KAP, ENT, SCO, SIB, PART, SEQ, RLY, HALF = range(11)
 
 
 def scan_device(block, core):
@@ -95,7 +95,7 @@
     y_out, r_out, s_out,
     q_in, k_in, v_in, go_in, res_in, dec_in, toe, mom, spr,
     x2, g2, prod, inn, y_acc, r_acc,
-    part_send, part_rcv,
+    part_send, part_rcv, half_rcv,
     mom_send, inn_send, prm_send,
     mom_rcv, inn_rcv, prm_rcv, kap_rcv, ent_rcv, sco_rcv, sib_rcv,
     psi, push, ebuf, before, ent_send, kap_send, sco_send, scalers,
@@ -134,18 +134,25 @@
 
     @pl.when(scans)
     def _():
-        def one(n, carry):
-            greet(lax.rem(me + n, DEVICES))
-            return carry
-
-        lax.fori_loop(1, DEVICES, one, 0)
-
-    @pl.when(jnp.logical_not(scans))
-    def _():
-        greet(sibling)
         for b in range(BLOCKS):
             for c in range(2):
-                greet(scan_device(b, c))
+                device = scan_device(b, c)
+
+                @pl.when(me != device)
+                def _():
+                    greet(device)
+
+        def one(n, carry):
+            z_there = lax.rem(Z_FIRST + 4 + lax.rem(lax.div(n, 4) + 4, 12), 16)
+            greet(lax.rem(n, 4) // 2 * 32 + z_there * 2 + lax.rem(n, 2))
+            return carry
+
+        lax.fori_loop(0, DEVICES - 2 * BLOCKS, one, 0)
+        pl.semaphore_wait(barrier, 2 * BLOCKS - 1)
+
+    @pl.when(jnp.logical_not(scans))
+    def _():
+        greet(sibling)
 
     def push_to(src, dst, kind, device):
         return pltpu.make_async_remote_copy(
@@ -200,10 +207,6 @@
     part_send[...] = jnp.where(first, of_g, of_x)
     kept = jnp.where(first, of_x, of_g)
 
-    @pl.when(scans)
-    def _():
-        pl.semaphore_wait(barrier, DEVICES - 1)
-
     @pl.when(jnp.logical_not(scans))
     def _():
         pl.semaphore_wait(barrier, 2 * BLOCKS + 1)
@@ -232,6 +235,13 @@
     moment_args = [(mom_send.at[b], mom_rcv.at[chip], MOM, scan_device(b, 0) + core) for b in range(BLOCKS)]
     for args in moment_args:
         send(*args)
+
+    @pl.when(jnp.logical_not(scans))
+    def _():
+        for b in range(BLOCKS):
+            for c in range(2):
+                greet(scan_device(b, c))
+
 
     loads[7].wait()
     loads[8].wait()
@@ -255,9 +265,19 @@
         return carry
 
     lax.fori_loop(0, 4, onward, 0)
-    for b in range(BLOCKS):
-        inn_send[b] = inn[:, b * SPAN : (b + 1) * SPAN].astype(BF16)
-    inner_args = [(inn_send.at[b], inn_rcv.at[me], INN, scan_device(b, 0)) for b in range(BLOCKS)]
+    wide = BLOCKS // 2 * SPAN
+    mine = pl.ds(pl.multiple_of(core * wide, wide), wide)
+    other = pl.ds(pl.multiple_of((1 - core) * wide, wide), wide)
+    half = push_to(inn.at[:, other], half_rcv, HALF, sibling)
+    half.start()
+    arrived(half_rcv, HALF)
+    inner = inn[:, mine] + half_rcv[...]
+    for b in range(BLOCKS // 2):
+        inn_send[b] = inner[:, b * SPAN : (b + 1) * SPAN].astype(BF16)
+    inner_args = [
+        (inn_send.at[b], inn_rcv.at[chip], INN, scanner_of(core * (BLOCKS // 2) + b, 0))
+        for b in range(BLOCKS // 2)
+    ]
     for args in inner_args:
         send(*args)
 
@@ -309,6 +329,8 @@
         kap_send[...] = kappa.astype(BF16)
         scalers[0], scalers[1] = scale, keep
 
+        pl.semaphore_wait(barrier, DEVICES - 2 * BLOCKS)
+
         def tell(n, carry):
             @pl.when(jnp.logical_or(lax.div(n, 2) < NEAR, lax.rem(lax.div(n, 2), 2) == core))
             def _():
@@ -328,7 +350,7 @@
             ebuf[b] = total
             return carry
 
-        lax.fori_loop(0, CHUNKS, expand, 0)
+        lax.fori_loop(0, CHUNKS, expand, 0, unroll=4)
 
         @pl.when(core == 1)
         def _():
@@ -345,7 +367,7 @@
             ent_send[b] = total.astype(BF16)
             return state * far + ebuf[b]
 
-        lax.fori_loop(0, CHUNKS, step, jnp.zeros((MODES, SPAN), F32))
+        lax.fori_loop(0, CHUNKS, step, jnp.zeros((MODES, SPAN), F32), unroll=4)
 
         def tell_entering(n, carry):
             b = by_z(n)
@@ -385,11 +407,10 @@
 
         def cross(b, carry):
             total, inner = carry
-            both = inn_rcv[2 * b].astype(F32) + inn_rcv[2 * b + 1].astype(F32)
-            return total + before[b] * sib_rcv[b], inner + both
+            return total + before[b] * sib_rcv[b], inner + inn_rcv[b].astype(F32)
 
         zero = jnp.zeros((MODES, SPAN), F32)
-        total, inner = lax.fori_loop(0, CHUNKS, cross, (zero, zero))
+        total, inner = lax.fori_loop(0, CHUNKS, cross, (zero, zero), unroll=4)
         total = total * keep
         for k in range(NODES):
             total = total + psi[k] * inner[k : k + 1, :]
@@ -427,6 +448,7 @@
     for args in moment_args + inner_args + param_args:
         sent(*args)
     part.wait_send()
+    half.wait_send()
 
     @pl.when(z >= NEAR)
     def _():
@@ -492,15 +514,15 @@
         vm((PAIR, channels), BF16), vm((PAIR, channels), BF16),
         vm((2, NODES * SPAN, channels), F32), vm((NODES, channels), F32),
         vm((tokens, channels), F32), vm((tokens, channels), F32),
-        vm((NODES, channels), F32), vm((NODES, channels), F32),
-        vm((BLOCKS, NODES, SPAN), BF16), vm((BLOCKS, NODES, SPAN), BF16), vm((4, SPAN), F32),
-        vm((CHUNKS, NODES, SPAN), BF16), vm((DEVICES, NODES, SPAN), BF16), vm((8, 4, SPAN), F32),
+        vm((NODES, channels), F32), vm((NODES, channels), F32), vm((NODES, channels // 2), F32),
+        vm((BLOCKS, NODES, SPAN), BF16), vm((BLOCKS // 2, NODES, SPAN), BF16), vm((4, SPAN), F32),
+        vm((CHUNKS, NODES, SPAN), BF16), vm((CHUNKS, NODES, SPAN), BF16), vm((8, 4, SPAN), F32),
         vm((BLOCKS, NODES, SPAN), BF16), vm((2, BLOCKS, NODES, SPAN), BF16), vm((MODES, SPAN), F32),
         vm((CHUNKS, MODES, SPAN), F32),
         vm((NODES, MODES, SPAN), F32), vm((MODES, NODES, SPAN), F32), vm((CHUNKS, MODES, SPAN), F32),
         vm((CHUNKS, MODES, SPAN), F32), vm((CHUNKS, NODES, SPAN), BF16), vm((NODES, SPAN), BF16),
         vm((MODES, SPAN), F32), vm((2, MODES, SPAN), F32),
-        pltpu.SemaphoreType.DMA((9,)), pltpu.SemaphoreType.DMA((10,)), pltpu.SemaphoreType.DMA((10,)),
+        pltpu.SemaphoreType.DMA((9,)), pltpu.SemaphoreType.DMA((11,)), pltpu.SemaphoreType.DMA((11,)),
     ]
     hbm = pl.BlockSpec(memory_space=pltpu.HBM)
     vmem = pl.BlockSpec(memory_space=pltpu.VMEM)

time: 35.9 us -> 33 us (0.919)
  Pallas kernels: 33.4 us -> 30.5 us
    pallas_call x1, Pallas kernels: 33.4 us -> 30.5 us  [body(): pl.pallas_call(kernel, out_shape=(jax.ShapeDtypeStruct((tokens, channels)...]
where the time goes in v3:
time: 33 us; the launch traced here: 32.9 us
  Pallas kernels  30.5 us (92%)
  other arithmetic  1.06 us (3%)
  between operations  0.69 us (2%)
  local copies, waits for them, and re-layouts  0.61 us (2%)
    pallas_call x1, Pallas kernels, body(): pl.pallas_call(kernel, out_shape=(jax.ShapeDtypeStruct((tokens, channels)...  30.5 us
    convert_element_type x1, other arithmetic, gated(): return (left.astype(F32) * right.astype(F32)).astype(BF16)  1.06 us

profile of v3, /device:TPU:1, one launch (start us, length us, event | category | flops | bytes accessed | tf_op | source)
XLA Modules:
  0.0 32.9 jit_solution(12014244314053169549)
XLA Ops:
  0.6 0.0 copy-start.2
  0.6 0.0 copy-start.1
  0.7 0.0 copy-start
  0.7 30.5 %chunk_convolution.1 = (bf16[128,1024]{1,0:T(8,128)(2,1)S(1)}, bf16[128,1024]{1,0:T(8,128)(2,1)S(1)}, f32[16,16]{1,0:T(8,128)S(1)}) custom-call(bf16[128,1024]{1,0:T(8,128)(2,1)} %q_hbm.1, bf16[128,1024]{1,0:T(8,128)(2,1)} %k_hbm.1, bf16[128,1024]{1,0:T(8,128)(2,1)} %v_hbm.1, bf16[128,1024]{1,0:T(8,128)(2,1)} %go_hbm.1, f32[16,16]{1,0:T(8,128)} %res_hbm.1, ...), custom_call_target="tpu_custom_call" | custom-call | flops 2147483648 | bytes 4194304 | tf_op jit(solution)/shard_map/chunk_convolution/pallas_call | solution.py:529
  31.2 0.0 copy-done.2
  31.2 0.0 copy-done.1
  31.2 0.0 copy-done
  31.2 1.1 %fusion.1 = (bf16[128,1024]{1,0:T(8,128)(2,1)}, bf16[128,1024]{1,0:T(8,128)(2,1)}, bf16[128,1024]{1,0:T(8,128)(2,1)}) fusion(bf16[128,1024]{1,0:T(8,128)(2,1)S(1)} %get-tuple-element.8, bf16[128,1024]{1,0:T(8,128)(2,1)S(1)} %copy-done, bf16[128,1024]{1,0:T(8,128)(2,1)S(1)} %copy-done.1, bf16[128,1024]{1,0:T(8,128)(2,1)S(1)} %get-tuple-element.7, ...), kind=kLoop, calls=%fused_computation.3 | loop fusion | flops 1441792 | bytes 2097152 | tf_op jit(solution)/shard_map/convert_element_type | solution.py:503
  32.3 0.6 %copy.14 = f32[16,16]{1,0:T(8,128)} copy(f32[16,16]{1,0:T(8,128)S(1)} %get-tuple-element.20) | data formatting | bytes 2048
Async XLA Ops:
  0.6 30.5 %copy-start.2 = (bf16[128,1024]{1,0:T(8,128)(2,1)S(1)}, bf16[128,1024]{1,0:T(8,128)(2,1)}, u32[]{:S(2)}) copy-start(bf16[128,1024]{1,0:T(8,128)(2,1)} %go_hbm.1) | copy-start | bytes 786436
  0.6 30.5 %copy-start.1 = (bf16[128,1024]{1,0:T(8,128)(2,1)S(1)}, bf16[128,1024]{1,0:T(8,128)(2,1)}, u32[]{:S(2)}) copy-start(bf16[128,1024]{1,0:T(8,128)(2,1)} %v_hbm.1) | copy-start | bytes 786436
  0.7 30.5 %copy-start = (bf16[128,1024]{1,0:T(8,128)(2,1)S(1)}, bf16[128,1024]{1,0:T(8,128)(2,1)}, u32[]{:S(2)}) copy-start(bf16[128,1024]{1,0:T(8,128)(2,1)} %k_hbm.1) | copy-start | bytes 786436

commit v4 on v3

--- a/solution.py
+++ b/solution.py
@@ -418,6 +418,50 @@
         for k in range(8):
             send(sco_send, sco_rcv, SCO, 8 * block + k)
 
+    for args in moment_args + inner_args + param_args:
+        sent(*args)
+    part.wait_send()
+    half.wait_send()
+
+    @pl.when(passes_taps)
+    def _():
+        push_to(kap_rcv, kap_rcv, KAP, sibling).wait_send()
+
+    @pl.when(first)
+    def _():
+        push_to(x2.at[pl.ds(0, SPAN)], x2.at[pl.ds(SPAN, SPAN)], SEQ, sibling).wait_send()
+
+    @pl.when(jnp.logical_not(first))
+    def _():
+        push_to(g2.at[pl.ds(0, SPAN)], g2.at[pl.ds(SPAN, SPAN)], SEQ, sibling).wait_send()
+
+    @pl.when(scans)
+    def _():
+        def told(n, carry):
+            @pl.when(jnp.logical_or(lax.div(n, 2) < NEAR, lax.rem(lax.div(n, 2), 2) == core))
+            def _():
+                sent(kap_send, kap_rcv.at[block], KAP, 2 * by_z(n) + core)
+
+            return carry
+
+        lax.fori_loop(0, CHUNKS, told, 0)
+
+        def stepped(n, carry):
+            b = by_z(n)
+            sent(ent_send.at[b], ent_rcv.at[core, block], ENT, 2 * b + core)
+
+            @pl.when(lax.div(n, 2) < NEAR)
+            def _():
+                sent(ent_send.at[b], ent_rcv.at[core, block], ENT, 2 * b + 1 - core)
+
+            return carry
+
+        lax.fori_loop(0, CHUNKS, stepped, 0)
+
+        @pl.when(core == 1)
+        def _():
+            push_to(ebuf, sib_rcv, SIB, me - 1).wait_send()
+
     near = z < NEAR
 
     @pl.when(near)
@@ -445,62 +489,36 @@
     turned = pltpu.roll(sco_rcv[...], lax.rem(SPAN - 16 * own_part, SPAN), 1)
     s_out[...] = jnp.transpose(turned)[:OWN, :]
 
-    for args in moment_args + inner_args + param_args:
-        sent(*args)
-    part.wait_send()
-    half.wait_send()
-
     @pl.when(z >= NEAR)
     def _():
         relay().wait_send()
 
-    @pl.when(passes_taps)
-    def _():
-        push_to(kap_rcv, kap_rcv, KAP, sibling).wait_send()
-
-    @pl.when(first)
-    def _():
-        push_to(x2.at[pl.ds(0, SPAN)], x2.at[pl.ds(SPAN, SPAN)], SEQ, sibling).wait_send()
-
-    @pl.when(jnp.logical_not(first))
-    def _():
-        push_to(g2.at[pl.ds(0, SPAN)], g2.at[pl.ds(SPAN, SPAN)], SEQ, sibling).wait_send()
-
-    @pl.when(scans)
-    def _():
-        def told(n, carry):
-            @pl.when(jnp.logical_or(lax.div(n, 2) < NEAR, lax.rem(lax.div(n, 2), 2) == core))
-            def _():
-                sent(kap_send, kap_rcv.at[block], KAP, 2 * by_z(n) + core)
-
-            return carry
-
-        lax.fori_loop(0, CHUNKS, told, 0)
-
-        def stepped(n, carry):
-            b = by_z(n)
-            sent(ent_send.at[b], ent_rcv.at[core, block], ENT, 2 * b + core)
-
-            @pl.when(lax.div(n, 2) < NEAR)
-            def _():
-                sent(ent_send.at[b], ent_rcv.at[core, block], ENT, 2 * b + 1 - core)
-
-            return carry
-
-        lax.fori_loop(0, CHUNKS, stepped, 0)
-
-        @pl.when(core == 1)
-        def _():
-            push_to(ebuf, sib_rcv, SIB, me - 1).wait_send()
-
-        @pl.when(core == 0)
-        def _():
-            for k in range(8):
-                sent(sco_send, sco_rcv, SCO, 8 * block + k)
-
-
-def gated(left, right):
-    return (left.astype(F32) * right.astype(F32)).astype(BF16)
+    @pl.when(jnp.logical_and(scans, first))
+    def _():
+        for k in range(8):
+            sent(sco_send, sco_rcv, SCO, 8 * block + k)
+
+
+def last_products(
+    y_ref, r_ref, go_ref, v_ref, k_ref, score_ref, gq_out, gk_out, gv_out, score_out, gq, gk, gv, score, sem
+):
+    score[...] = score_ref[...]
+    copies = [pltpu.make_async_copy(score, score_out, sem.at[0])]
+    copies[0].start()
+    rows = 32
+    for n in range(SPAN // rows):
+        part = pl.ds(n * rows, rows)
+        y = y_ref[part, :].astype(F32)
+        r = r_ref[part, :].astype(F32)
+        for c, (mine, gate, left, out) in enumerate(
+            ((gq, go_ref, y, gq_out), (gk, v_ref, r, gk_out), (gv, k_ref, r, gv_out))
+        ):
+            mine[part, :] = (left * gate[part, :].astype(F32)).astype(BF16)
+            copy = pltpu.make_async_copy(mine.at[part], out.at[part], sem.at[1 + 3 * n + c])
+            copy.start()
+            copies.append(copy)
+    for copy in copies:
+        copy.wait()
 
 
 def body(query_gate, key_gate, value_input, grad_out, residues, decay):
@@ -543,12 +561,16 @@
         name="chunk_convolution",
     )(*(pltpu.with_memory_space_constraint(a, pltpu.HBM) for a in (
         query_gate, key_gate, value_input, grad_out, residues, decay, toeplitz, moments, spread)))
-    return (
-        gated(grad_out, output),
-        gated(backward, value_input),
-        gated(backward, key_gate),
-        score,
-    )
+    wide = jax.ShapeDtypeStruct((tokens, channels), BF16)
+    return pl.pallas_call(
+        last_products,
+        out_shape=(wide, wide, wide, jax.ShapeDtypeStruct((OWN, MODES), F32)),
+        in_specs=[vmem] * 6,
+        out_specs=(pl.BlockSpec(memory_space=pl.ANY),) * 4,
+        scratch_shapes=[gate, gate, gate, vm((OWN, MODES), F32), pltpu.SemaphoreType.DMA((13,))],
+        compiler_params=pltpu.CompilerParams(vmem_limit_bytes=8 * 2**20),
+        name="last_products",
+    )(output, backward, grad_out, value_input, key_gate, score)
 
 
 def solution(mesh):

time: 33 us -> 31.4 us (0.952)
  other arithmetic: 1.06 us -> 0 us
  local copies, waits for them, and re-layouts: 0.61 us -> 0.01 us
    convert_element_type x1 -> x0, other arithmetic: 1.06 us -> none  [gated(): return (left.astype(F32) * right.astype(F32)).astype(BF16)]
    pallas_call x0 -> x1, Pallas kernels: none -> 1 us  [body(): pl.pallas_call(last_products, out_shape=(wide, wide, wide, jax.ShapeDtype...]
    pallas_call x1, Pallas kernels: 30.5 us -> 29.6 us  [body(): pl.pallas_call(kernel, out_shape=(jax.ShapeDtypeStruct((tokens, channels)...]
    unnamed x7 -> x6, local copies, waits for them, and re-layouts: 0.61 us -> 0.01 us
where the time goes in v4:
time: 31.4 us; the launch traced here: 31.3 us
  Pallas kernels  30.6 us (97%)
  between operations  0.69 us (2%)
    pallas_call x1, Pallas kernels, body(): pl.pallas_call(kernel, out_shape=(jax.ShapeDtypeStruct((tokens, channels)...  29.6 us
    pallas_call x1, Pallas kernels, body(): pl.pallas_call(last_products, out_shape=(wide, wide, wide, jax.ShapeDtype...  1 us

profile of v4, /device:TPU:1, one launch (start us, length us, event | category | flops | bytes accessed | tf_op | source)
XLA Modules:
  0.0 31.3 jit_solution(7714140476010144978)
XLA Ops:
  0.6 0.0 copy-start.2
  0.6 0.0 copy-start.1
  0.7 0.0 copy-start
  0.7 29.6 %chunk_convolution.1 = (bf16[128,1024]{1,0:T(8,128)(2,1)S(1)}, bf16[128,1024]{1,0:T(8,128)(2,1)S(1)}, f32[16,16]{1,0:T(8,128)S(1)}) custom-call(bf16[128,1024]{1,0:T(8,128)(2,1)} %q_hbm.1, bf16[128,1024]{1,0:T(8,128)(2,1)} %k_ref.1, bf16[128,1024]{1,0:T(8,128)(2,1)} %v_ref.1, bf16[128,1024]{1,0:T(8,128)(2,1)} %go_ref.1, f32[16,16]{1,0:T(8,128)} %res_hbm.1, ...), custom_call_target="tpu_custom_call" | custom-call | flops 2147483648 | bytes 4194304 | tf_op jit(solution)/shard_map/chunk_convolution/pallas_call | solution.py:547
  30.2 0.0 copy-done.2
  30.2 0.0 copy-done.1
  30.3 0.0 copy-done
  30.3 1.0 %last_products.1 = (bf16[128,1024]{1,0:T(8,128)(2,1)}, bf16[128,1024]{1,0:T(8,128)(2,1)}, bf16[128,1024]{1,0:T(8,128)(2,1)}, f32[16,16]{1,0:T(8,128)}) custom-call(bf16[128,1024]{1,0:T(8,128)(2,1)S(1)} %get-tuple-element.7.y_ref, bf16[128,1024]{1,0:T(8,128)(2,1)S(1)} %get-tuple-element.8.r_ref, bf16[128,1024]{1,0:T(8,128)(2,1)S(1)} %copy-done.2, ...), custom_call_target="tpu_custom_call" | custom-call | tf_op jit(solution)/shard_map/last_products/pallas_call | solution.py:565
Async XLA Ops:
  0.6 29.6 %copy-start.2 = (bf16[128,1024]{1,0:T(8,128)(2,1)S(1)}, bf16[128,1024]{1,0:T(8,128)(2,1)}, u32[]{:S(2)}) copy-start(bf16[128,1024]{1,0:T(8,128)(2,1)} %go_ref.1) | copy-start | bytes 786436
  0.6 29.6 %copy-start.1 = (bf16[128,1024]{1,0:T(8,128)(2,1)S(1)}, bf16[128,1024]{1,0:T(8,128)(2,1)}, u32[]{:S(2)}) copy-start(bf16[128,1024]{1,0:T(8,128)(2,1)} %v_ref.1) | copy-start | bytes 786436
  0.7 29.6 %copy-start = (bf16[128,1024]{1,0:T(8,128)(2,1)S(1)}, bf16[128,1024]{1,0:T(8,128)(2,1)}, u32[]{:S(2)}) copy-start(bf16[128,1024]{1,0:T(8,128)(2,1)} %k_ref.1) | copy-start | bytes 786436

commit v5 on v4

--- a/solution.py
+++ b/solution.py
@@ -23,7 +23,7 @@
 OWN = 16
 BEND = 200.0
 Z_FIRST, Z_STEP = 0, 1
-NEAR = 4
+NEAR = 2
 MOM, INN, PRM, KAP, ENT, SCO, SIB, PART, SEQ, RLY, HALF = range(11)
 
 
@@ -195,17 +195,13 @@
         loads[n].wait()
     x = (k_in[...].astype(F32) * v_in[...].astype(F32)).astype(BF16)
     g = (go_in[...].astype(F32) * q_in[...].astype(F32)).astype(BF16)
-    x2[:SPAN, :] = x
-    g2[:SPAN, :] = g
+    first = core == 0
 
     def moment(c, value):
         both = jnp.dot(mom[2 * core + c], value, preferred_element_type=F32)
         return both[:NODES] + both[NODES:]
 
-    of_x, of_g = moment(0, x), moment(1, g)
-    first = core == 0
-    part_send[...] = jnp.where(first, of_g, of_x)
-    kept = jnp.where(first, of_x, of_g)
+    part_send[...] = moment(1 - core, jnp.where(first, g, x))
 
     @pl.when(jnp.logical_not(scans))
     def _():
@@ -217,6 +213,9 @@
 
     part = push_to(part_send, part_rcv, PART, sibling)
     part.start()
+    kept = moment(core, jnp.where(first, x, g))
+    x2[:SPAN, :] = x
+    g2[:SPAN, :] = g
 
     @pl.when(first)
     def _():
@@ -292,7 +291,7 @@
         return i + core * (CHUNKS - 1 - 2 * i)
 
     def by_z(n):
-        return lax.rem(n, 2) * 16 + lax.div(n, 2)
+        return lax.rem(n + 1 + y_hi, 2) * 16 + lax.div(n, 2)
 
     @pl.when(scans)
     def _():

time: 31.4 us -> 31.4 us (level)
  no operation moved by 1% of the time
where the time goes in v5:
time: 31.4 us; the launch traced here: 31.3 us
  Pallas kernels  30.6 us (97%)
  between operations  0.69 us (2%)
    pallas_call x1, Pallas kernels, body(): pl.pallas_call(kernel, out_shape=(jax.ShapeDtypeStruct((tokens, channels)...  29.6 us
    pallas_call x1, Pallas kernels, body(): pl.pallas_call(last_products, out_shape=(wide, wide, wide, jax.ShapeDtype...  1 us

profile of v5, /device:TPU:1, one launch (start us, length us, event | category | flops | bytes accessed | tf_op | source)
XLA Modules:
  0.0 31.3 jit_solution(9790588254628215573)
XLA Ops:
  0.6 0.0 copy-start.2
  0.6 0.0 copy-start.1
  0.7 0.0 copy-start
  0.7 29.6 %chunk_convolution.1 = (bf16[128,1024]{1,0:T(8,128)(2,1)S(1)}, bf16[128,1024]{1,0:T(8,128)(2,1)S(1)}, f32[16,16]{1,0:T(8,128)S(1)}) custom-call(bf16[128,1024]{1,0:T(8,128)(2,1)} %q_hbm.1, bf16[128,1024]{1,0:T(8,128)(2,1)} %k_ref.1, bf16[128,1024]{1,0:T(8,128)(2,1)} %v_ref.1, bf16[128,1024]{1,0:T(8,128)(2,1)} %go_ref.1, f32[16,16]{1,0:T(8,128)} %res_hbm.1, ...), custom_call_target="tpu_custom_call" | custom-call | flops 2147483648 | bytes 4194304 | tf_op jit(solution)/shard_map/chunk_convolution/pallas_call | solution.py:546
  30.2 0.0 copy-done.2
  30.3 0.0 copy-done.1
  30.3 0.0 copy-done
  30.3 1.0 %last_products.1 = (bf16[128,1024]{1,0:T(8,128)(2,1)}, bf16[128,1024]{1,0:T(8,128)(2,1)}, bf16[128,1024]{1,0:T(8,128)(2,1)}, f32[16,16]{1,0:T(8,128)}) custom-call(bf16[128,1024]{1,0:T(8,128)(2,1)S(1)} %get-tuple-element.7.y_ref, bf16[128,1024]{1,0:T(8,128)(2,1)S(1)} %get-tuple-element.8.r_ref, bf16[128,1024]{1,0:T(8,128)(2,1)S(1)} %copy-done.2, ...), custom_call_target="tpu_custom_call" | custom-call | tf_op jit(solution)/shard_map/last_products/pallas_call | solution.py:564
Async XLA Ops:
  0.6 29.6 %copy-start.2 = (bf16[128,1024]{1,0:T(8,128)(2,1)S(1)}, bf16[128,1024]{1,0:T(8,128)(2,1)}, u32[]{:S(2)}) copy-start(bf16[128,1024]{1,0:T(8,128)(2,1)} %go_ref.1) | copy-start | bytes 786436
  0.6 29.6 %copy-start.1 = (bf16[128,1024]{1,0:T(8,128)(2,1)S(1)}, bf16[128,1024]{1,0:T(8,128)(2,1)}, u32[]{:S(2)}) copy-start(bf16[128,1024]{1,0:T(8,128)(2,1)} %v_ref.1) | copy-start | bytes 786436
  0.7 29.6 %copy-start = (bf16[128,1024]{1,0:T(8,128)(2,1)S(1)}, bf16[128,1024]{1,0:T(8,128)(2,1)}, u32[]{:S(2)}) copy-start(bf16[128,1024]{1,0:T(8,128)(2,1)} %k_ref.1) | copy-start | bytes 786436

commit v6 on v5

--- a/solution.py
+++ b/solution.py
@@ -337,7 +337,7 @@
 
             return carry
 
-        lax.fori_loop(0, CHUNKS, tell, 0)
+        lax.fori_loop(0, CHUNKS, tell, 0, unroll=4)
 
         arrived(mom_rcv, MOM)
 
@@ -378,7 +378,7 @@
 
             return carry
 
-        lax.fori_loop(0, CHUNKS, tell_entering, 0)
+        lax.fori_loop(0, CHUNKS, tell_entering, 0, unroll=4)
 
     arrived(kap_rcv, KAP)
     passes_taps = jnp.logical_and(z >= NEAR, lax.rem(z, 2) == core)

time: 31.4 us -> 31.4 us (level)
  no operation moved by 1% of the time
where the time goes in v6:
time: 31.4 us; the launch traced here: 31.3 us
  Pallas kernels  30.6 us (97%)
  between operations  0.69 us (2%)
    pallas_call x1, Pallas kernels, body(): pl.pallas_call(kernel, out_shape=(jax.ShapeDtypeStruct((tokens, channels)...  29.6 us
    pallas_call x1, Pallas kernels, body(): pl.pallas_call(last_products, out_shape=(wide, wide, wide, jax.ShapeDtype...  1 us

profile of v6, /device:TPU:1, one launch (start us, length us, event | category | flops | bytes accessed | tf_op | source)
XLA Modules:
  0.0 31.3 jit_solution(8556750249934103576)
XLA Ops:
  0.6 0.0 copy-start.2
  0.6 0.0 copy-start.1
  0.7 0.0 copy-start
  0.7 29.6 %chunk_convolution.1 = (bf16[128,1024]{1,0:T(8,128)(2,1)S(1)}, bf16[128,1024]{1,0:T(8,128)(2,1)S(1)}, f32[16,16]{1,0:T(8,128)S(1)}) custom-call(bf16[128,1024]{1,0:T(8,128)(2,1)} %q_hbm.1, bf16[128,1024]{1,0:T(8,128)(2,1)} %k_ref.1, bf16[128,1024]{1,0:T(8,128)(2,1)} %v_ref.1, bf16[128,1024]{1,0:T(8,128)(2,1)} %go_ref.1, f32[16,16]{1,0:T(8,128)} %res_hbm.1, ...), custom_call_target="tpu_custom_call" | custom-call | flops 2147483648 | bytes 4194304 | tf_op jit(solution)/shard_map/chunk_convolution/pallas_call | solution.py:546
  30.2 0.0 copy-done.2
  30.3 0.0 copy-done.1
  30.3 0.0 copy-done
  30.3 1.0 %last_products.1 = (bf16[128,1024]{1,0:T(8,128)(2,1)}, bf16[128,1024]{1,0:T(8,128)(2,1)}, bf16[128,1024]{1,0:T(8,128)(2,1)}, f32[16,16]{1,0:T(8,128)}) custom-call(bf16[128,1024]{1,0:T(8,128)(2,1)S(1)} %get-tuple-element.7.y_ref, bf16[128,1024]{1,0:T(8,128)(2,1)S(1)} %get-tuple-element.8.r_ref, bf16[128,1024]{1,0:T(8,128)(2,1)S(1)} %copy-done.2, ...), custom_call_target="tpu_custom_call" | custom-call | tf_op jit(solution)/shard_map/last_products/pallas_call | solution.py:564
Async XLA Ops:
  0.6 29.6 %copy-start.2 = (bf16[128,1024]{1,0:T(8,128)(2,1)S(1)}, bf16[128,1024]{1,0:T(8,128)(2,1)}, u32[]{:S(2)}) copy-start(bf16[128,1024]{1,0:T(8,128)(2,1)} %go_ref.1) | copy-start | bytes 786436
  0.6 29.6 %copy-start.1 = (bf16[128,1024]{1,0:T(8,128)(2,1)S(1)}, bf16[128,1024]{1,0:T(8,128)(2,1)}, u32[]{:S(2)}) copy-start(bf16[128,1024]{1,0:T(8,128)(2,1)} %v_ref.1) | copy-start | bytes 786436
  0.7 29.6 %copy-start = (bf16[128,1024]{1,0:T(8,128)(2,1)S(1)}, bf16[128,1024]{1,0:T(8,128)(2,1)}, u32[]{:S(2)}) copy-start(bf16[128,1024]{1,0:T(8,128)(2,1)} %k_ref.1) | copy-start | bytes 786436
